TPU v7x, 512 devices: a whole 4x8x8 slice. The times are simulated.
512 devices in a mesh: row: 16 (over x_lo, y), col: 32 (over z, x_hi, core).
Axes of the slice: x: 4 (x_hi: 2, x_lo: 2; x = x_hi * 2 + x_lo), y: 8, z: 8, core: 2. Of those that a mesh axis runs over, the one named last changes fastest.
Arguments:
- inputs: bfloat16 [512, 12288], P('col', 'row'), may hold values from -6 to 6
- w_up: bfloat16 [12288, 24576], P('row', 'col'), may hold values from -0.0546875 to 0.0546875
- w_down: bfloat16 [24576, 12288], P('col', 'row'), may hold values from -0.0390625 to 0.0390625
- grad_out: bfloat16 [512, 12288], P('col', 'row'), may hold values from -1.5 to 1.5
Outputs:
- grad_in: bfloat16 [512, 12288], P('col', 'row')
- grad_up: bfloat16 [12288, 24576], P('row', 'col')
- grad_down: bfloat16 [24576, 12288], P('col', 'row')
All inputs are finite; a program needn't handle non-finite values.
Results may differ from a plain program's by a relative error of at most 0.0049.
Values may be sent and summed in bfloat16 or wider, within the bound.
No kernel may reach another device: no remote copies, remote signals or barrier semaphores. Data moves between devices by JAX's collectives and lax.ppermute only.
A program may use at most 64 MiB of HBM per device.

v0:
```python
import math

import jax
import jax.numpy as jnp
from jax import lax
from jax.sharding import PartitionSpec as P

gelu_scale = math.sqrt(2.0 / math.pi)
cubic_coef = 0.044715


def gelu_parts(pre_act):
    tangent = jnp.tanh(gelu_scale * (pre_act + cubic_coef * pre_act * pre_act * pre_act))
    gelu_value = 0.5 * pre_act * (1.0 + tangent)
    gelu_slope = 0.5 * (1.0 + tangent) + 0.5 * pre_act * (1.0 - tangent * tangent) * gelu_scale * (
        1.0 + 3.0 * cubic_coef * pre_act * pre_act
    )
    return (gelu_value, gelu_slope)


def per_device(inputs, w_up, w_down, grad_out):
    whole_in, whole_grad = (
        lax.all_gather(inputs, "col", axis=0, tiled=True),
        lax.all_gather(grad_out, "col", axis=0, tiled=True),
    )
    pre_term = jnp.dot(whole_in, w_up, preferred_element_type=jnp.float32)
    back_term = lax.dot_general(
        whole_grad, w_down, (((1,), (1,)), ((), ())), preferred_element_type=jnp.float32
    )
    pre_full, back_full = lax.psum((pre_term, back_term), "row")
    gelu_value, gelu_slope = gelu_parts(pre_full)
    act_rows = gelu_value.astype(jnp.bfloat16)
    dpre_rows = (back_full * gelu_slope).astype(jnp.bfloat16)
    grad_up = lax.dot_general(
        whole_in, dpre_rows, (((0,), (0,)), ((), ())), preferred_element_type=jnp.float32
    )
    grad_down = lax.dot_general(
        act_rows, whole_grad, (((0,), (0,)), ((), ())), preferred_element_type=jnp.float32
    )
    grad_in = lax.psum_scatter(
        lax.dot_general(
            dpre_rows, w_up, (((1,), (1,)), ((), ())), preferred_element_type=jnp.float32
        ),
        "col",
        scatter_dimension=0,
        tiled=True,
    )
    return (
        grad_in.astype(jnp.bfloat16),
        grad_up.astype(jnp.bfloat16),
        grad_down.astype(jnp.bfloat16),
    )


def solution(mesh):
    in_specs = (P("col", "row"), P("row", "col"), P("col", "row"), P("col", "row"))
    out_specs = (P("col", "row"), P("row", "col"), P("col", "row"))
    return jax.shard_map(
        per_device, mesh=mesh, in_specs=in_specs, out_specs=out_specs, check_vma=False
    )
```

profile of v0, /device:TPU:8, one launch (start us, length us, event | category | flops | bytes accessed | tf_op | source)
XLA Modules:
  0.0 388.0 jit_solution(14156428208422721834)
XLA Ops:
  7.2 0.0 copy-start
  7.2 0.0 all-reduce.3.cloned.1.call-start
  7.2 0.0 copy-start.2
  7.2 50.4 %all_gather.7 = bf16[512,768]{1,0:T(8,128)(2,1)S(1)} all-gather(bf16[16,768]{1,0:T(8,128)(2,1)} %param.4), channel_id=1, replica_groups=mesh['row'=16,'col'=32] {'col'}, dimensions={0}, use_global_device_ids=true | all-gather | bytes 811008 | tf_op jit(solution)/shard_map/all_gather | solution.py:23
  57.7 39.2 %all_gather.6 = bf16[512,768]{1,0:T(8,128)(2,1)S(1)} all-gather(bf16[16,768]{1,0:T(8,128)(2,1)} %param.7), channel_id=1, replica_groups=mesh['row'=16,'col'=32] {'col'}, dimensions={0}, use_global_device_ids=true | all-gather | bytes 811008 | tf_op jit(solution)/shard_map/all_gather | solution.py:24
  96.8 0.0 copy-done.2
  96.8 2.0 fusion.16
  98.8 0.0 copy-done
  98.8 1.9 fusion.17
  100.8 0.0 all-reduce.3.cloned.1.call-update
  100.8 0.0 reduce-scatter.2.cloned.1.call-start
  100.8 149.0 %all-reduce.3.cloned.1.call-done = (f32[512,768]{1,0:T(8,128)}, f32[512,768]{1,0:T(8,128)}) async-done(((f32[512,768]{1,0:T(8,128)}, f32[512,768]{1,0:T(8,128)}), (f32[512,768]{1,0:T(8,128)}, f32[512,768]{1,0:T(8,128)})) %all-reduce.3.cloned.1.call-update) | async-done | bytes 3145744 | tf_op jit(solution)/shard_map/psum | solution.py:30
  249.8 2.9 fusion.6
  252.7 2.0 fusion.18
  254.7 0.0 reduce-scatter.2.cloned.1.call-update
  254.7 1.8 fusion.7
  256.5 0.0 copy-start.1
  256.5 2.5 copy.7
  259.0 0.0 copy-done.1
  259.0 2.0 convolution_convert_fusion
  261.0 118.8 %reduce-scatter.2.cloned.1.call-done = f32[16,768]{1,0:T(8,128)} async-done(((f32[512,768]{1,0:T(8,128)}), f32[16,768]{1,0:T(8,128)}) %reduce-scatter.2.cloned.1.call-update) | async-done | bytes 49168 | tf_op jit(solution)/shard_map/reduce_scatter | solution.py:40
  379.8 1.4 convert_element_type.19
Async XLA Ops:
  7.2 91.6 %copy-start = (bf16[768,768]{1,0:T(8,128)(2,1)S(1)}, bf16[768,768]{1,0:T(8,128)(2,1)}, u32[]{:S(2)}) copy-start(bf16[768,768]{1,0:T(8,128)(2,1)} %param.5) | copy-start | bytes 3538948
  7.2 242.7 %all-reduce.3.cloned.1.call-start = ((), (), s32[]{:S(2)}) async-start(), calls=%async_computation.2 | async-start | bytes 6291456 | tf_op jit(solution)/shard_map/psum | solution.py:30
  7.2 89.6 %copy-start.2 = (bf16[768,768]{1,0:T(8,128)(2,1)S(1)}, bf16[768,768]{1,0:T(8,128)(2,1)}, u32[]{:S(2)}) copy-start(bf16[768,768]{1,0:T(8,128)(2,1)} %param.6) | copy-start | bytes 3538948
  100.8 279.0 %reduce-scatter.2.cloned.1.call-start = ((), (), s32[]{:S(2)}) async-start(), calls=%async_computation.1 | async-start | bytes 1622016 | tf_op jit(solution)/shard_map/reduce_scatter | solution.py:40
  256.5 2.5 copy-start.1
Sparse Core Ops, SparseCore 0:
  100.9 148.9 all-reduce.2
  254.8 124.9 reduce-scatter.1
where the time goes:
time: 388 us
  waiting for transfers between devices  268 us (69%)
  blocking collectives  89.6 us (23%)
  between operations  14.1 us (4%)
  matrix products  9.65 us (2%)
  other arithmetic  4.28 us (1%)
    psum x1, waiting for transfers between devices, per_device(): pre_full, back_full = lax.psum((pre_term, back_term), 'row')  149 us
    reduce_scatter x1, waiting for transfers between devices, per_device(): lax.psum_scatter(lax.dot_general(dpre_rows, w_up, (((1,), (1,)), ((), ())...  119 us
    all_gather x1, blocking collectives, per_device(): lax.all_gather(inputs, 'col', axis=0, tiled=True)  50.4 us
    all_gather x1, blocking collectives, per_device(): lax.all_gather(grad_out, 'col', axis=0, tiled=True)  39.2 us
  transfers between devices with their start and end apart: 2, of which 2 were waited for; matrix products, arithmetic and copies ran while one was open for 2% of the time, Pallas kernels for 0%

commit v1 on v0

v1 whole, which is shorter than its diff:
```python
import math

import jax
import jax.numpy as jnp
from jax import lax
from jax.sharding import Mesh, PartitionSpec as P

gelu_scale = math.sqrt(2.0 / math.pi)
cubic_coef = 0.044715


def gelu_parts(pre_act):
    tangent = jnp.tanh(gelu_scale * (pre_act + cubic_coef * pre_act * pre_act * pre_act))
    gelu_value = 0.5 * pre_act * (1.0 + tangent)
    gelu_slope = 0.5 * (1.0 + tangent) + 0.5 * pre_act * (1.0 - tangent * tangent) * gelu_scale * (
        1.0 + 3.0 * cubic_coef * pre_act * pre_act
    )
    return (gelu_value, gelu_slope)


ROW = ("xl", "y")


def swap(blocks, axes):
    return lax.all_to_all(blocks, axes, split_axis=0, concat_axis=0, tiled=True)


def spread(block, axes, size):
    copies = jnp.broadcast_to(block[None], (size,) + block.shape)
    return swap(copies.reshape((size * block.shape[0],) + block.shape[1:]), axes)


def per_device(inputs, w_up, w_down, grad_out):
    f32, bf16 = jnp.float32, jnp.bfloat16
    tokens, width = inputs.shape
    hidden = w_up.shape[1]
    both = spread(jnp.concatenate([inputs, grad_out], axis=0), "z", 8)
    both = lax.all_gather(both, "xh", axis=0, tiled=True).reshape(16, 2, tokens, width)
    whole_in = lax.all_gather(both[:, 0].reshape(-1, width), "c", axis=0, tiled=True)
    whole_grad = lax.all_gather(both[:, 1].reshape(-1, width), "c", axis=0, tiled=True)

    pre_term = jnp.dot(whole_in, w_up, preferred_element_type=f32).astype(bf16)
    back_term = lax.dot_general(
        whole_grad, w_down, (((1,), (1,)), ((), ())), preferred_element_type=f32
    ).astype(bf16)
    terms = jnp.stack(
        [pre_term.reshape(16, -1, hidden), back_term.reshape(16, -1, hidden)], axis=1
    )
    terms = swap(terms.reshape(-1, hidden), ROW).reshape(16, 2, -1, hidden)
    sums = jnp.sum(terms.astype(f32), axis=0)
    gelu_value, gelu_slope = gelu_parts(sums[0])
    mine = jnp.concatenate(
        [gelu_value.astype(bf16), (sums[1] * gelu_slope).astype(bf16)], axis=0
    )
    full = spread(mine, ROW, 16).reshape(16, 2, -1, hidden)
    act, dpre = full[:, 0].reshape(-1, hidden), full[:, 1].reshape(-1, hidden)

    partial_in = lax.dot_general(
        dpre, w_up, (((1,), (1,)), ((), ())), preferred_element_type=f32
    )
    halves = swap(partial_in, "c").reshape(2, -1, width)
    halves = (halves[0] + halves[1]).astype(bf16)
    pieces = swap(halves, ("xh", "z")).reshape(16, -1, width)
    grad_in = jnp.sum(pieces.astype(f32), axis=0).astype(bf16)

    grad_up = lax.dot_general(
        whole_in, dpre, (((0,), (0,)), ((), ())), preferred_element_type=f32
    )
    grad_down = lax.dot_general(
        act, whole_grad, (((0,), (0,)), ((), ())), preferred_element_type=f32
    )
    return (grad_in, grad_up.astype(bf16), grad_down.astype(bf16))


def solution(mesh):
    fine = Mesh(mesh.devices.reshape(2, 8, 8, 2, 2), ("xl", "y", "z", "xh", "c"))
    row, col = ("xl", "y"), ("z", "xh", "c")
    in_specs = (P(col, row), P(row, col), P(col, row), P(col, row))
    out_specs = (P(col, row), P(row, col), P(col, row))
    return jax.shard_map(
        per_device, mesh=fine, in_specs=in_specs, out_specs=out_specs, check_vma=False
    )
```

time: 388 us -> 163 us (0.42)
  waiting for transfers between devices: 268 us -> 9.71 us
  blocking collectives: 89.6 us -> 135 us
  between operations: 14.1 us -> 0.73 us
  starting transfers between devices: 0.08 us -> 5.21 us
    psum x1 -> x0, waiting for transfers between devices: 149 us -> none  [per_device(): pre_full, back_full = lax.psum((pre_term, back_term), 'row')]
    reduce_scatter x1 -> x0, waiting for transfers between devices: 119 us -> none  [per_device(): lax.psum_scatter(lax.dot_general(dpre_rows, w_up, (((1,), (1,)), ((), ())...]
    all_to_all x0 -> x4, blocking collectives: none -> 118 us  [swap(): return lax.all_to_all(blocks, axes, split_axis=0, concat_axis=0, tiled=True)]
    all_gather x2 -> x3, blocking collectives: 89.6 us -> 16.3 us  [the longest x1 11.6 us: per_device(): lax.all_gather(both, 'xh', axis=0, tiled=True).reshape(16, 2, tokens, width)]
    all_to_all x0 -> x1, waiting for transfers between devices: none -> 9.71 us  [swap(): return lax.all_to_all(blocks, axes, split_axis=0, concat_axis=0, tiled=True)]
    all_to_all x0 -> x1, starting transfers between devices: none -> 5.21 us  [swap(): return lax.all_to_all(blocks, axes, split_axis=0, concat_axis=0, tiled=True)]
  transfers between devices with their start and end apart: 2 -> 1, of which waited for: 2 -> 1; matrix products, arithmetic and copies ran while one was open for 2% -> 3% of each run, Pallas kernels for 0% -> 0%
where the time goes in v1:
time: 163 us; the launch traced here: 162 us
  blocking collectives  135 us (83%)
  waiting for transfers between devices  9.71 us (6%)
  matrix products  7.25 us (4%)
  starting transfers between devices  5.21 us (3%)
  other arithmetic  2.79 us (2%)
  local copies, waits for them, and re-layouts  1.79 us (1%)
    all_to_all x4, blocking collectives, swap(): return lax.all_to_all(blocks, axes, split_axis=0, concat_axis=0, tiled=True)  118 us
    all_gather x1, blocking collectives, per_device(): lax.all_gather(both, 'xh', axis=0, tiled=True).reshape(16, 2, tokens, width)  11.6 us
    all_to_all x1, waiting for transfers between devices, swap(): return lax.all_to_all(blocks, axes, split_axis=0, concat_axis=0, tiled=True)  9.71 us
    all_to_all x1, starting transfers between devices, swap(): return lax.all_to_all(blocks, axes, split_axis=0, concat_axis=0, tiled=True)  5.21 us
  transfers between devices with their start and end apart: 1, of which 1 were waited for; matrix products, arithmetic and copies ran while one was open for 3% of the time, Pallas kernels for 0%

profile of v1, /device:TPU:8, one launch (start us, length us, event | category | flops | bytes accessed | tf_op | source)
XLA Modules:
  0.0 162.2 jit_solution(13305118087215923850)
XLA Ops:
  0.6 0.0 copy-start
  0.6 0.9 pad_maximum_fusion.2
  1.5 24.8 %all_to_all.36 = bf16[8,32,768]{2,1,0:T(8,128)(2,1)S(1)} all-to-all(bf16[8,32,768]{2,1,0:T(8,128)(2,1)S(1)} %broadcast_in_dim.4), channel_id=1, replica_groups=mesh['xl'=2,'y'=8,'z'=8,'xh'=2,'c'=2] {'z'}, dimensions={0} | all-to-all | bytes 786432 | tf_op jit(solution)/shard_map/all_to_all | solution.py:25
  26.3 11.6 %all_gather.9 = bf16[512,768]{1,0:T(8,128)(2,1)S(1)} all-gather(bf16[256,768]{1,0:T(8,128)(2,1)S(1)} %bitcast.31), channel_id=1, replica_groups=mesh['xl'=2,'y'=8,'z'=8,'xh'=2,'c'=2] {'xh'}, dimensions={0}, use_global_device_ids=true | all-gather | bytes 1179648 | tf_op jit(solution)/shard_map/all_gather | solution.py:38
  37.9 0.1 fusion.11
  38.0 2.4 %all_gather.11 = bf16[512,768]{1,0:T(8,128)(2,1)S(1)} all-gather(bf16[256,768]{1,0:T(8,128)(2,1)S(1)} %bitcast.33), channel_id=1, replica_groups=mesh['xl'=2,'y'=8,'z'=8,'xh'=2,'c'=2] {'c'}, dimensions={0}, use_global_device_ids=true | all-gather | bytes 1179648 | tf_op jit(solution)/shard_map/all_gather | solution.py:40
  40.3 2.4 %all_gather.10 = bf16[512,768]{1,0:T(8,128)(2,1)S(1)} all-gather(bf16[256,768]{1,0:T(8,128)(2,1)S(1)} %bitcast.32), channel_id=1, replica_groups=mesh['xl'=2,'y'=8,'z'=8,'xh'=2,'c'=2] {'c'}, dimensions={0}, use_global_device_ids=true | all-gather | bytes 1179648 | tf_op jit(solution)/shard_map/all_gather | solution.py:39
  42.7 0.0 copy-done
  42.7 0.0 copy-start.3
  42.7 0.8 convolution_convert_fusion.3
  43.5 0.5 copy-done.3
  44.0 0.8 convolution_convert_fusion.2
  44.8 0.2 pad_maximum_fusion
  44.9 46.4 %all_to_all.37 = bf16[16,64,768]{2,1,0:T(8,128)(2,1)S(1)} all-to-all(bf16[16,64,768]{2,1,0:T(8,128)(2,1)S(1)} %bitcast.29), channel_id=1, replica_groups=mesh['xl'=2,'y'=8,'z'=8,'xh'=2,'c'=2] {'xl','y'}, dimensions={0} | all-to-all | bytes 3145728 | tf_op jit(solution)/shard_map/all_to_all | solution.py:25
  91.3 0.2 convert_reduce_fusion
  91.5 0.1 multiply_convert_fusion
  91.6 0.1 broadcast_in_dim.5
  91.8 42.3 %all_to_all.38 = bf16[16,64,768]{2,1,0:T(8,128)(2,1)S(1)} all-to-all(bf16[16,64,768]{2,1,0:T(8,128)(2,1)S(1)} %broadcast_in_dim.5), channel_id=1, replica_groups=mesh['xl'=2,'y'=8,'z'=8,'xh'=2,'c'=2] {'xl','y'}, dimensions={0} | all-to-all | bytes 3145728 | tf_op jit(solution)/shard_map/all_to_all | solution.py:25
  134.0 1.0 fusion.10
  135.0 0.0 copy-start.1
  135.0 0.8 fusion
  135.8 0.1 copy-done.1
  135.9 5.0 %all_to_all.39 = f32[2,256,768]{2,1,0:T(8,128)S(1)} all-to-all(f32[2,256,768]{2,1,0:T(8,128)S(1)} %fusion), channel_id=1, replica_groups=mesh['xl'=2,'y'=8,'z'=8,'xh'=2,'c'=2] {'c'}, dimensions={0} | all-to-all | bytes 3145728 | tf_op jit(solution)/shard_map/all_to_all | solution.py:25
  140.9 0.8 fusion.2
  141.7 5.2 %all-to-all-start.4 = ((bf16[16,16,768]{2,1,0:T(8,128)(2,1)}), bf16[16,16,768]{2,1,0:T(8,128)(2,1)S(1)}, u32[]{:S(2)}, u32[]{:S(2)}) async-start(bf16[16,16,768]{2,1,0:T(8,128)(2,1)} %bitcast.12), calls=%async_computation.4 | async-start | bytes 786432 | tf_op jit(solution)/shard_map/all_to_all | solution.py:25
  146.9 0.0 copy-start.2
  146.9 3.0 %convolution_convert_fusion = bf16[768,768]{1,0:T(8,128)(2,1)} fusion(bf16[512,768]{1,0:T(8,128)(2,1)} %bitcast.36, bf16[512,768]{1,0:T(8,128)(2,1)S(1)} %all_gather.11), kind=kOutput, calls=%fused_computation.2 | convolution fusion | flops 604569600 | bytes 2752512 | tf_op jit(solution)/shard_map/dot_general | solution.py:69
  150.0 0.0 copy-done.2
  150.0 1.8 %convolution_convert_fusion.1 = bf16[768,768]{1,0:T(8,128)(2,1)} fusion(bf16[512,768]{1,0:T(8,128)(2,1)S(1)} %all_gather.10, bf16[512,768]{1,0:T(8,128)(2,1)S(1)} %bitcast.35), kind=kOutput, calls=%fused_computation.3 | convolution fusion | flops 604569600 | bytes 2752512 | tf_op jit(solution)/shard_map/dot_general | solution.py:66
  151.8 9.7 %all-to-all-done.4 = bf16[16,16,768]{2,1,0:T(8,128)(2,1)S(1)} async-done(((bf16[16,16,768]{2,1,0:T(8,128)(2,1)}), bf16[16,16,768]{2,1,0:T(8,128)(2,1)S(1)}, u32[]{:S(2)}, u32[]{:S(2)}) %all-to-all-start.4) | async-done | bytes 393248 | tf_op jit(solution)/shard_map/all_to_all | solution.py:25
  161.5 0.7 reduce_sum.22
  (2 shorter events, 0.0 us)
Async XLA Ops:
  0.6 42.1 %copy-start = (bf16[768,768]{1,0:T(8,128)(2,1)S(1)}, bf16[768,768]{1,0:T(8,128)(2,1)}, u32[]{:S(2)}) copy-start(bf16[768,768]{1,0:T(8,128)(2,1)} %param.5) | copy-start | bytes 3538948
  42.7 1.3 copy-start.3
  135.0 0.9 copy-start.1
  141.7 19.8 %all-to-all-start.4 = ((bf16[16,16,768]{2,1,0:T(8,128)(2,1)}), bf16[16,16,768]{2,1,0:T(8,128)(2,1)S(1)}, u32[]{:S(2)}, u32[]{:S(2)}) async-start(bf16[16,16,768]{2,1,0:T(8,128)(2,1)} %bitcast.12), calls=%async_computation.4 | async-start | bytes 786432 | tf_op jit(solution)/shard_map/all_to_all | solution.py:25
  146.9 3.0 %copy-start.2 = (bf16[16,1,32,768]{3,2,1,0:T(8,128)(2,1)S(1)}, bf16[16,1,32,768]{3,2,1,0:T(8,128)(2,1)}, u32[]{:S(2)}) copy-start(bf16[16,1,32,768]{3,2,1,0:T(8,128)(2,1)} %copy-done.1) | copy-start | bytes 2359300

commit v2 on v1

v2 whole, which is shorter than its diff:
```python
import math

import jax
import jax.numpy as jnp
from jax import lax
from jax.sharding import Mesh, PartitionSpec as P

gelu_scale = math.sqrt(2.0 / math.pi)
cubic_coef = 0.044715


def gelu_parts(pre_act):
    tangent = jnp.tanh(gelu_scale * (pre_act + cubic_coef * pre_act * pre_act * pre_act))
    gelu_value = 0.5 * pre_act * (1.0 + tangent)
    gelu_slope = 0.5 * (1.0 + tangent) + 0.5 * pre_act * (1.0 - tangent * tangent) * gelu_scale * (
        1.0 + 3.0 * cubic_coef * pre_act * pre_act
    )
    return (gelu_value, gelu_slope)


def swap(blocks, axes):
    return lax.all_to_all(blocks, axes, split_axis=0, concat_axis=0, tiled=True)


def spread(block, axes, size):
    copies = jnp.broadcast_to(block[None], (size,) + block.shape)
    return swap(copies.reshape((size * block.shape[0],) + block.shape[1:]), axes)


def gather(block, axis):
    return lax.all_gather(block, axis, axis=0, tiled=True)


def other(block, axis):
    return lax.ppermute(block, axis, [(0, 1), (1, 0)])


def per_device(inputs, w_up, w_down, grad_out):
    f32, bf16 = jnp.float32, jnp.bfloat16
    tokens, width = inputs.shape
    hidden = w_up.shape[1]
    xl, xh, core = lax.axis_index("xl"), lax.axis_index("xh"), lax.axis_index("c")

    def over_cores(part):
        part = gather(part, "c").reshape(16, 2, tokens, width)
        return part[:, 0].reshape(-1, width), part[:, 1].reshape(-1, width)

    def half(rows, which):
        size = rows.shape[0] // 2
        return lax.dynamic_slice_in_dim(rows, which * size, size, 0)

    def pre_and_back(whole_in, whole_grad, which):
        return jnp.stack(
            [
                jnp.dot(half(whole_in, which), w_up, preferred_element_type=f32),
                lax.dot_general(
                    half(whole_grad, which),
                    w_down,
                    (((1,), (1,)), ((), ())),
                    preferred_element_type=f32,
                ),
            ]
        )

    def pair_sums(whole_in, whole_grad):
        got = other(pre_and_back(whole_in, whole_grad, 1 - xl).astype(bf16), "xl")
        sums = pre_and_back(whole_in, whole_grad, xl) + got.astype(f32)
        return sums.astype(bf16).reshape(2, 8, tokens, hidden)

    def row_sums(pairs):
        pieces = swap(jnp.swapaxes(pairs, 0, 1).reshape(-1, hidden), "y")
        return jnp.sum(pieces.reshape(8, 2, tokens, hidden).astype(f32), axis=0)

    near = spread(jnp.concatenate([inputs, grad_out], axis=0), "z", 8)
    far = other(near, "xh")
    near_in, near_grad = over_cores(near)
    near_sums = row_sums(pair_sums(near_in, near_grad))
    far_in, far_grad = over_cores(far)
    far_sums = row_sums(pair_sums(far_in, far_grad))

    pre = jnp.concatenate([near_sums[0], far_sums[0]], axis=0)
    back = jnp.concatenate([near_sums[1], far_sums[1]], axis=0)
    gelu_value, gelu_slope = gelu_parts(pre)
    dpre_mine = spread((back * gelu_slope).astype(bf16), "y", 8)
    dpre_mine, act_rows = lax.optimization_barrier((dpre_mine, gelu_value.astype(bf16)))
    dpre_other = other(dpre_mine, "xl")
    act_mine = spread(act_rows, "y", 8)

    def in_of(rows):
        return lax.dot_general(
            rows, w_up, (((1,), (1,)), ((), ())), preferred_element_type=f32
        )

    from_mine, from_other = in_of(dpre_mine), in_of(dpre_other)
    same = core == xl
    kept = jnp.where(same, from_mine, from_other)
    given = jnp.where(same, from_other, from_mine)
    given, act_mine = lax.optimization_barrier((given, act_mine))
    act_other = other(act_mine, "xl")
    kept = (kept + other(given, "c")).astype(bf16).reshape(8, 2, tokens, width)
    first = xh == 0
    kept = jnp.stack(
        [
            jnp.where(first, kept[:, 0], kept[:, 1]),
            jnp.where(first, kept[:, 1], kept[:, 0]),
        ]
    ).reshape(-1, width)
    pieces = swap(kept, ("xh", "z")).reshape(16, tokens, width)
    grad_in = jnp.sum(pieces.astype(f32), axis=0).astype(bf16)

    def by_half(near, far):
        rows = [x.reshape(2, 8, tokens, width) for x in (near, far)]
        rows = jnp.stack(rows, axis=2).reshape(2, -1, width)
        return (
            lax.dynamic_index_in_dim(rows, xl, 0, False),
            lax.dynamic_index_in_dim(rows, 1 - xl, 0, False),
        )

    def over_tokens(left, right):
        return lax.dot_general(
            left, right, (((0,), (0,)), ((), ())), preferred_element_type=f32
        )

    in_mine, in_other = by_half(near_in, far_in)
    grad_mine, grad_other = by_half(near_grad, far_grad)
    grad_up = over_tokens(in_mine, dpre_mine) + over_tokens(in_other, dpre_other)
    grad_down = over_tokens(act_mine, grad_mine) + over_tokens(act_other, grad_other)
    return (grad_in, grad_up.astype(bf16), grad_down.astype(bf16))


def solution(mesh):
    fine = Mesh(mesh.devices.reshape(2, 8, 8, 2, 2), ("xl", "y", "z", "xh", "c"))
    row, col = ("xl", "y"), ("z", "xh", "c")
    in_specs = (P(col, row), P(row, col), P(col, row), P(col, row))
    out_specs = (P(col, row), P(row, col), P(col, row))
    return jax.shard_map(
        per_device, mesh=fine, in_specs=in_specs, out_specs=out_specs, check_vma=False
    )
```

time: 163 us -> 156 us (0.957)
  the two profiles are of different devices: /device:TPU:8 before, /device:TPU:1 now
where the time goes in v2:
time: 156 us; the launch traced here: 155 us
  starting transfers between devices  55 us (35%)
  waiting for transfers between devices  50.9 us (33%)
  blocking collectives  21.9 us (14%)
  matrix products  14.3 us (9%)
  other arithmetic  8.11 us (5%)
  local copies, waits for them, and re-layouts  3.63 us (2%)
    all_to_all x5, waiting for transfers between devices, swap(): return lax.all_to_all(blocks, axes, split_axis=0, concat_axis=0, tiled=True)  38.7 us
    all_to_all x5, starting transfers between devices, swap(): return lax.all_to_all(blocks, axes, split_axis=0, concat_axis=0, tiled=True)  32.1 us
    ppermute x6, starting transfers between devices, other(): return lax.ppermute(block, axis, [(0, 1), (1, 0)])  22.9 us
    all_to_all x1, blocking collectives, swap(): return lax.all_to_all(blocks, axes, split_axis=0, concat_axis=0, tiled=True)  13.4 us
    ppermute x6, waiting for transfers between devices, other(): return lax.ppermute(block, axis, [(0, 1), (1, 0)])  12.2 us
    all_gather x2, blocking collectives, gather(): return lax.all_gather(block, axis, axis=0, tiled=True)  8.52 us
    dot_general x4, matrix products, over_tokens(): lax.dot_general(left, right, (((0,), (0,)), ((), ())), preferred_element_...  7.29 us
  transfers between devices with their start and end apart: 11, of which 9 were waited for; matrix products, arithmetic and copies ran while one was open for 14% of the time, Pallas kernels for 0%

profile of v2, /device:TPU:1, one launch (start us, length us, event | category | flops | bytes accessed | tf_op | source)
XLA Modules:
  0.0 154.8 jit_solution(6497687662858838455)
XLA Ops:
  0.6 0.9 pad_maximum_fusion.6
  1.5 0.8 broadcast_in_dim.6
  2.3 10.9 %all-to-all-start = ((bf16[8,32,768]{2,1,0:T(8,128)(2,1)}), bf16[8,32,768]{2,1,0:T(8,128)(2,1)S(1)}, u32[]{:S(2)}, u32[]{:S(2)}) async-start(bf16[8,32,768]{2,1,0:T(8,128)(2,1)} %broadcast_in_dim.6), calls=%async_computation | async-start | bytes 786432 | tf_op jit(solution)/shard_map/all_to_all | solution.py:22
  13.1 14.2 %all-to-all-done = bf16[8,32,768]{2,1,0:T(8,128)(2,1)S(1)} async-done(((bf16[8,32,768]{2,1,0:T(8,128)(2,1)}), bf16[8,32,768]{2,1,0:T(8,128)(2,1)S(1)}, u32[]{:S(2)}, u32[]{:S(2)}) %all-to-all-start) | async-done | bytes 393248 | tf_op jit(solution)/shard_map/all_to_all | solution.py:22
  27.3 4.8 %collective-permute-start.1 = (bf16[256,768]{1,0:T(8,128)(2,1)S(1)}, bf16[256,768]{1,0:T(8,128)(2,1)S(1)}, u32[]{:S(2)}, u32[]{:S(2)}) collective-permute-start(bf16[256,768]{1,0:T(8,128)(2,1)S(1)} %bitcast.118), channel_id=1, source_target_pairs={{0,2},{2,0},{1,3},{3,1},{4,6},{6,4},{5,7},{7,5},{8,10},{10,8},{9,1... | collective-permute-start | bytes 1179656 | tf_op jit(solution)/shard_map/ppermute | solution.py:35
  32.1 3.7 %all_gather.6 = bf16[512,768]{1,0:T(8,128)(2,1)S(1)} all-gather(bf16[256,768]{1,0:T(8,128)(2,1)S(1)} %bitcast.119), channel_id=1, replica_groups=mesh['xl'=2,'y'=8,'z'=8,'xh'=2,'c'=2] {'c'}, dimensions={0}, use_global_device_ids=true | all-gather | bytes 1179648 | tf_op jit(solution)/shard_map/all_gather | solution.py:31
  35.9 0.5 fusion.1
  36.5 0.3 fusion
  36.8 2.2 %collective-permute-start = (bf16[2,128,768]{2,1,0:T(8,128)(2,1)S(1)}, bf16[2,128,768]{2,1,0:T(8,128)(2,1)S(1)}, u32[]{:S(2)}, u32[]{:S(2)}) collective-permute-start(bf16[2,128,768]{2,1,0:T(8,128)(2,1)S(1)} %pad_maximum_fusion.2), channel_id=1, source_target_pairs={{0,256},{256,0},{1,257},{257,1},{2,258},{258,2},{3,259},{259,3},{4... | collective-permute-start | bytes 1179656 | tf_op jit(solution)/shard_map/ppermute | solution.py:35
  39.1 0.5 convolution_bitcast_fusion.2
  39.6 0.3 convolution_bitcast_fusion.3
  40.0 4.8 %all_gather.7 = bf16[512,768]{1,0:T(8,128)(2,1)S(1)} all-gather(bf16[256,768]{1,0:T(8,128)(2,1)S(1)} %collective-permute-done.1), channel_id=1, replica_groups=mesh['xl'=2,'y'=8,'z'=8,'xh'=2,'c'=2] {'c'}, dimensions={0}, use_global_device_ids=true | all-gather | bytes 1179648 | tf_op jit(solution)/shard_map/all_gather | solution.py:31
  44.9 1.2 fusion.3
  46.1 1.0 fusion.2
  47.2 2.8 %collective-permute-done = bf16[2,128,768]{2,1,0:T(8,128)(2,1)S(1)} collective-permute-done((bf16[2,128,768]{2,1,0:T(8,128)(2,1)S(1)}, bf16[2,128,768]{2,1,0:T(8,128)(2,1)S(1)}, u32[]{:S(2)}, u32[]{:S(2)}) %collective-permute-start) | collective-permute-done | bytes 393248 | tf_op jit(solution)/shard_map/ppermute | solution.py:35
  50.0 0.8 copy.17
  50.8 6.8 %all-to-all-start.1 = ((bf16[8,32,768]{2,1,0:T(8,128)(2,1)}), bf16[8,32,768]{2,1,0:T(8,128)(2,1)}, u32[]{:S(2)}, u32[]{:S(2)}) async-start(bf16[8,32,768]{2,1,0:T(8,128)(2,1)} %bitcast.116), calls=%async_computation.1 | async-start | bytes 786432 | tf_op jit(solution)/shard_map/all_to_all | solution.py:22
  57.6 1.1 pad_maximum_fusion.3
  58.7 2.2 %collective-permute-start.2 = (bf16[2,128,768]{2,1,0:T(8,128)(2,1)S(1)}, bf16[2,128,768]{2,1,0:T(8,128)(2,1)S(1)}, u32[]{:S(2)}, u32[]{:S(2)}) collective-permute-start(bf16[2,128,768]{2,1,0:T(8,128)(2,1)S(1)} %pad_maximum_fusion.3), channel_id=1, source_target_pairs={{0,256},{256,0},{1,257},{257,1},{2,258},{258,2},{3,259},{259,3},{4... | collective-permute-start | bytes 1179656 | tf_op jit(solution)/shard_map/ppermute | solution.py:35
  61.0 0.5 convolution_bitcast_fusion
  61.5 0.3 convolution_bitcast_fusion.1
  61.8 8.1 %collective-permute-done.2 = bf16[2,128,768]{2,1,0:T(8,128)(2,1)S(1)} collective-permute-done((bf16[2,128,768]{2,1,0:T(8,128)(2,1)S(1)}, bf16[2,128,768]{2,1,0:T(8,128)(2,1)S(1)}, u32[]{:S(2)}, u32[]{:S(2)}) %collective-permute-start.2) | collective-permute-done | bytes 393248 | tf_op jit(solution)/shard_map/ppermute | solution.py:35
  70.1 0.8 copy.18
  70.8 0.2 all-to-all-done.1
  71.1 6.1 %all-to-all-start.2 = ((bf16[8,32,768]{2,1,0:T(8,128)(2,1)}), bf16[8,32,768]{2,1,0:T(8,128)(2,1)S(1)}, u32[]{:S(2)}, u32[]{:S(2)}) async-start(bf16[8,32,768]{2,1,0:T(8,128)(2,1)} %bitcast.20), calls=%async_computation.2 | async-start | bytes 786432 | tf_op jit(solution)/shard_map/all_to_all | solution.py:22
  77.2 1.1 convert_reduce_fusion.1
  78.3 10.4 %all-to-all-done.2 = bf16[8,32,768]{2,1,0:T(8,128)(2,1)S(1)} async-done(((bf16[8,32,768]{2,1,0:T(8,128)(2,1)}), bf16[8,32,768]{2,1,0:T(8,128)(2,1)S(1)}, u32[]{:S(2)}, u32[]{:S(2)}) %all-to-all-start.2) | async-done | bytes 393248 | tf_op jit(solution)/shard_map/all_to_all | solution.py:22
  88.9 13.4 %all_to_all.54 = bf16[8,32,768]{2,1,0:T(8,128)(2,1)S(1)} all-to-all(bf16[8,32,768]{2,1,0:T(8,128)(2,1)S(1)} %broadcast_in_dim.7), channel_id=1, replica_groups=mesh['xl'=2,'y'=8,'z'=8,'xh'=2,'c'=2] {'y'}, dimensions={0} | all-to-all | bytes 786432 | tf_op jit(solution)/shard_map/all_to_all | solution.py:22
  102.3 1.9 %collective-permute-start.3 = (bf16[256,768]{1,0:T(8,128)(2,1)S(1)}, bf16[256,768]{1,0:T(8,128)(2,1)S(1)}, u32[]{:S(2)}, u32[]{:S(2)}) collective-permute-start(bf16[256,768]{1,0:T(8,128)(2,1)S(1)} %bitcast.93), channel_id=1, source_target_pairs={{0,256},{256,0},{1,257},{257,1},{2,258},{258,2},{3,259},{259,3},{4... | collective-permute-start | bytes 1179656 | tf_op jit(solution)/shard_map/ppermute | solution.py:35
  104.2 0.8 broadcast_in_dim.8
  105.0 4.1 %all-to-all-start.4 = ((bf16[8,32,768]{2,1,0:T(8,128)(2,1)}), bf16[8,32,768]{2,1,0:T(8,128)(2,1)}, u32[]{:S(2)}, u32[]{:S(2)}) async-start(bf16[8,32,768]{2,1,0:T(8,128)(2,1)} %broadcast_in_dim.8), calls=%async_computation.4 | async-start | bytes 786432 | tf_op jit(solution)/shard_map/all_to_all | solution.py:22
  109.1 0.5 fusion.49
  109.6 1.2 collective-permute-done.3
  110.8 1.7 %broadcast_select_fusion = (f32[256,768]{1,0:T(8,128)}, f32[256,768]{1,0:T(8,128)}) fusion(f32[256,768]{1,0:T(8,128)S(1)} %fusion.49, pred[]{:T(512)S(6)} %eq.7, bf16[256,768]{1,0:T(8,128)(2,1)S(1)} %collective-permute-done.3, bf16[768,768]{1,0:T(8,128)(2,1)S(1)} %copy-done), kind=kOutput, calls=%fused_computation.37 | convolution fusion | flops 302186496 | bytes 3932161 | tf_op jit(solution)/shard_map/dot_general | solution.py:90
  112.4 7.5 %all-to-all-done.4 = bf16[8,32,768]{2,1,0:T(8,128)(2,1)} async-done(((bf16[8,32,768]{2,1,0:T(8,128)(2,1)}), bf16[8,32,768]{2,1,0:T(8,128)(2,1)}, u32[]{:S(2)}, u32[]{:S(2)}) %all-to-all-start.4) | async-done | bytes 393248 | tf_op jit(solution)/shard_map/all_to_all | solution.py:22
  119.9 8.1 %collective-permute-start.4 = (f32[256,768]{1,0:T(8,128)}, f32[256,768]{1,0:T(8,128)}, u32[]{:S(2)}, u32[]{:S(2)}) collective-permute-start(f32[256,768]{1,0:T(8,128)} %get-tuple-element.9), channel_id=1, source_target_pairs={{0,1},{1,0},{2,3},{3,2},{4,5},{5,4},{6,7},{7,6},{8,9},{9,8},{10,11... | collective-permute-start | bytes 2359304 | tf_op jit(solution)/shard_map/ppermute | solution.py:35
  128.1 1.0 pad_maximum_fusion.1
  129.1 0.3 copy-done.5
  129.4 0.5 fusion.10
  129.9 3.6 %collective-permute-start.5 = (bf16[256,768]{1,0:T(8,128)(2,1)}, bf16[256,768]{1,0:T(8,128)(2,1)}, u32[]{:S(2)}, u32[]{:S(2)}) collective-permute-start(bf16[256,768]{1,0:T(8,128)(2,1)} %bitcast.22), channel_id=1, source_target_pairs={{0,256},{256,0},{1,257},{257,1},{2,258},{258,2},{3,259},{259,3},{4... | collective-permute-start | bytes 1179656 | tf_op jit(solution)/shard_map/ppermute | solution.py:35
  133.6 1.2 add_convert_fusion.2
  134.9 0.8 pad_maximum_fusion.4
  135.7 4.2 %all-to-all-start.5 = ((bf16[16,16,768]{2,1,0:T(8,128)(2,1)}), bf16[16,16,768]{2,1,0:T(8,128)(2,1)}, u32[]{:S(2)}, u32[]{:S(2)}) async-start(bf16[16,16,768]{2,1,0:T(8,128)(2,1)} %bitcast.117), calls=%async_computation.5 | async-start | bytes 786432 | tf_op jit(solution)/shard_map/all_to_all | solution.py:22
  139.9 2.7 %add_convert_fusion.1 = bf16[768,768]{1,0:T(8,128)(2,1)} fusion(f32[768,768]{1,0:T(8,128)S(1)} %fusion.10, bf16[256,768]{1,0:T(8,128)(2,1)} %copy-done.12, bf16[2,256,768]{2,1,0:T(8,128)(2,1)} %bitcast.115, s32[]{:T(128)S(6)} %select_n.76), kind=kOutput, calls=%fused_computation.1 | convolution fusion | flops 303169536 | bytes 4325380 | tf_op jit(solution)/shard_map/dot_general | solution.py:120
  142.7 1.5 fusion.7
  144.2 2.5 %add_convert_fusion = bf16[768,768]{1,0:T(8,128)(2,1)} fusion(f32[768,768]{1,0:T(8,128)S(1)} %fusion.7, bf16[256,768]{1,0:T(8,128)(2,1)} %collective-permute-done.5, bf16[2,256,768]{2,1,0:T(8,128)(2,1)S(1)} %bitcast.113, s32[]{:T(128)S(6)} %select_n.76), kind=kOutput, calls=%fused_computation | convolution fusion | flops 303169536 | bytes 4325380 | tf_op jit(solution)/shard_map/dot_general | solution.py:120
  146.7 6.4 %all-to-all-done.5 = bf16[16,16,768]{2,1,0:T(8,128)(2,1)} async-done(((bf16[16,16,768]{2,1,0:T(8,128)(2,1)}), bf16[16,16,768]{2,1,0:T(8,128)(2,1)}, u32[]{:S(2)}, u32[]{:S(2)}) %all-to-all-start.5) | async-done | bytes 393248 | tf_op jit(solution)/shard_map/all_to_all | solution.py:22
  153.1 1.7 %reduce_sum.32 = bf16[16,768]{1,0:T(8,128)(2,1)} reduce(bf16[16,16,768]{2,1,0:T(8,128)(2,1)} %all-to-all-done.5, bf16[]{:T(256)} %constant.42.clone.1), dimensions={0}, to_apply=%region_2.3 | reduce | flops 184320 | bytes 417794 | tf_op jit(solution)/shard_map/reduce_sum | solution.py:109
  (41 shorter events, 0.7 us)
Async XLA Ops:
  0.6 35.8 %copy-start = (bf16[768,768]{1,0:T(8,128)(2,1)S(1)}, bf16[768,768]{1,0:T(8,128)(2,1)}, u32[]{:S(2)}) copy-start(bf16[768,768]{1,0:T(8,128)(2,1)} %param.5) | copy-start | bytes 3538948
  2.3 25.1 %all-to-all-start = ((bf16[8,32,768]{2,1,0:T(8,128)(2,1)}), bf16[8,32,768]{2,1,0:T(8,128)(2,1)S(1)}, u32[]{:S(2)}, u32[]{:S(2)}) async-start(bf16[8,32,768]{2,1,0:T(8,128)(2,1)} %broadcast_in_dim.6), calls=%async_computation | async-start | bytes 786432 | tf_op jit(solution)/shard_map/all_to_all | solution.py:22
  27.3 8.6 %copy-start.1 = (bf16[768,768]{1,0:T(8,128)(2,1)S(1)}, bf16[768,768]{1,0:T(8,128)(2,1)}, u32[]{:S(2)}) copy-start(bf16[768,768]{1,0:T(8,128)(2,1)} %param.6) | copy-start | bytes 3538948
  27.3 12.7 %collective-permute-start.1 = (bf16[256,768]{1,0:T(8,128)(2,1)S(1)}, bf16[256,768]{1,0:T(8,128)(2,1)S(1)}, u32[]{:S(2)}, u32[]{:S(2)}) collective-permute-start(bf16[256,768]{1,0:T(8,128)(2,1)S(1)} %bitcast.118), channel_id=1, source_target_pairs={{0,2},{2,0},{1,3},{3,1},{4,6},{6,4},{5,7},{7,5},{8,10},{10,8},{9,1... | collective-permute-start | bytes 1179656 | tf_op jit(solution)/shard_map/ppermute | solution.py:35
  36.8 13.1 %collective-permute-start = (bf16[2,128,768]{2,1,0:T(8,128)(2,1)S(1)}, bf16[2,128,768]{2,1,0:T(8,128)(2,1)S(1)}, u32[]{:S(2)}, u32[]{:S(2)}) collective-permute-start(bf16[2,128,768]{2,1,0:T(8,128)(2,1)S(1)} %pad_maximum_fusion.2), channel_id=1, source_target_pairs={{0,256},{256,0},{1,257},{257,1},{2,258},{258,2},{3,259},{259,3},{4... | collective-permute-start | bytes 1179656 | tf_op jit(solution)/shard_map/ppermute | solution.py:35
  44.9 2.3 %copy-start.6 = (bf16[16,1,16,768]{3,2,1,0:T(8,128)(2,1)}, bf16[16,1,16,768]{3,2,1,0:T(8,128)(2,1)S(1)}, u32[]{:S(2)}) copy-start(bf16[16,1,16,768]{3,2,1,0:T(8,128)(2,1)S(1)} %get-tuple-element.13) | copy-start | bytes 1179652
  50.8 20.3 %all-to-all-start.1 = ((bf16[8,32,768]{2,1,0:T(8,128)(2,1)}), bf16[8,32,768]{2,1,0:T(8,128)(2,1)}, u32[]{:S(2)}, u32[]{:S(2)}) async-start(bf16[8,32,768]{2,1,0:T(8,128)(2,1)} %bitcast.116), calls=%async_computation.1 | async-start | bytes 786432 | tf_op jit(solution)/shard_map/all_to_all | solution.py:22
  57.6 3.9 %copy-start.7 = (bf16[16,1,16,768]{3,2,1,0:T(8,128)(2,1)S(1)}, bf16[16,1,16,768]{3,2,1,0:T(8,128)(2,1)}, u32[]{:S(2)}) copy-start(bf16[16,1,16,768]{3,2,1,0:T(8,128)(2,1)} %copy-done.6) | copy-start | bytes 1179652
  58.7 11.3 %collective-permute-start.2 = (bf16[2,128,768]{2,1,0:T(8,128)(2,1)S(1)}, bf16[2,128,768]{2,1,0:T(8,128)(2,1)S(1)}, u32[]{:S(2)}, u32[]{:S(2)}) collective-permute-start(bf16[2,128,768]{2,1,0:T(8,128)(2,1)S(1)} %pad_maximum_fusion.3), channel_id=1, source_target_pairs={{0,256},{256,0},{1,257},{257,1},{2,258},{258,2},{3,259},{259,3},{4... | collective-permute-start | bytes 1179656 | tf_op jit(solution)/shard_map/ppermute | solution.py:35
  71.1 17.6 %all-to-all-start.2 = ((bf16[8,32,768]{2,1,0:T(8,128)(2,1)}), bf16[8,32,768]{2,1,0:T(8,128)(2,1)S(1)}, u32[]{:S(2)}, u32[]{:S(2)}) async-start(bf16[8,32,768]{2,1,0:T(8,128)(2,1)} %bitcast.20), calls=%async_computation.2 | async-start | bytes 786432 | tf_op jit(solution)/shard_map/all_to_all | solution.py:22
  102.3 7.3 %copy-start.4 = (bf16[8,32,768]{2,1,0:T(8,128)(2,1)}, bf16[8,32,768]{2,1,0:T(8,128)(2,1)S(1)}, u32[]{:S(2)}) copy-start(bf16[8,32,768]{2,1,0:T(8,128)(2,1)S(1)} %all_to_all.54) | copy-start | bytes 1179652
  102.3 8.5 %collective-permute-start.3 = (bf16[256,768]{1,0:T(8,128)(2,1)S(1)}, bf16[256,768]{1,0:T(8,128)(2,1)S(1)}, u32[]{:S(2)}, u32[]{:S(2)}) collective-permute-start(bf16[256,768]{1,0:T(8,128)(2,1)S(1)} %bitcast.93), channel_id=1, source_target_pairs={{0,256},{256,0},{1,257},{257,1},{2,258},{258,2},{3,259},{259,3},{4... | collective-permute-start | bytes 1179656 | tf_op jit(solution)/shard_map/ppermute | solution.py:35
  105.0 14.9 %all-to-all-start.4 = ((bf16[8,32,768]{2,1,0:T(8,128)(2,1)}), bf16[8,32,768]{2,1,0:T(8,128)(2,1)}, u32[]{:S(2)}, u32[]{:S(2)}) async-start(bf16[8,32,768]{2,1,0:T(8,128)(2,1)} %broadcast_in_dim.8), calls=%async_computation.4 | async-start | bytes 786432 | tf_op jit(solution)/shard_map/all_to_all | solution.py:22
  109.6 1.2 copy-start.2
  109.6 18.4 %copy-start.8 = (bf16[16,1,16,768]{3,2,1,0:T(8,128)(2,1)S(1)}, bf16[16,1,16,768]{3,2,1,0:T(8,128)(2,1)}, u32[]{:S(2)}) copy-start(bf16[16,1,16,768]{3,2,1,0:T(8,128)(2,1)} %copy-done.6) | copy-start | bytes 1179652
  110.8 18.3 %copy-start.12 = (bf16[256,768]{1,0:T(8,128)(2,1)}, bf16[256,768]{1,0:T(8,128)(2,1)S(1)}, u32[]{:S(2)}) copy-start(bf16[256,768]{1,0:T(8,128)(2,1)S(1)} %collective-permute-done.3) | copy-start | bytes 1179652
  119.9 13.7 %collective-permute-start.4 = (f32[256,768]{1,0:T(8,128)}, f32[256,768]{1,0:T(8,128)}, u32[]{:S(2)}, u32[]{:S(2)}) collective-permute-start(f32[256,768]{1,0:T(8,128)} %get-tuple-element.9), channel_id=1, source_target_pairs={{0,1},{1,0},{2,3},{3,2},{4,5},{5,4},{6,7},{7,6},{8,9},{9,8},{10,11... | collective-permute-start | bytes 2359304 | tf_op jit(solution)/shard_map/ppermute | solution.py:35
  128.1 5.5 %copy-start.10 = (bf16[2,8,2,16,768]{4,3,2,1,0:T(8,128)(2,1)}, bf16[2,8,2,16,768]{4,3,2,1,0:T(8,128)(2,1)S(1)}, u32[]{:S(2)}) copy-start(bf16[2,8,2,16,768]{4,3,2,1,0:T(8,128)(2,1)S(1)} %pad_maximum_fusion) | copy-start | bytes 2359300
  128.1 1.3 copy-start.5
  129.4 4.2 %copy-start.3 = (f32[256,768]{1,0:T(8,128)S(1)}, f32[256,768]{1,0:T(8,128)}, u32[]{:S(2)}) copy-start(f32[256,768]{1,0:T(8,128)} %copy-done.2) | copy-start | bytes 2359300
  129.4 4.2 %copy-start.11 = (f32[256,768]{1,0:T(8,128)S(1)}, f32[256,768]{1,0:T(8,128)}, u32[]{:S(2)}) copy-start(f32[256,768]{1,0:T(8,128)} %get-tuple-element.22) | copy-start | bytes 2359300
  129.9 14.3 %collective-permute-start.5 = (bf16[256,768]{1,0:T(8,128)(2,1)}, bf16[256,768]{1,0:T(8,128)(2,1)}, u32[]{:S(2)}, u32[]{:S(2)}) collective-permute-start(bf16[256,768]{1,0:T(8,128)(2,1)} %bitcast.22), channel_id=1, source_target_pairs={{0,256},{256,0},{1,257},{257,1},{2,258},{258,2},{3,259},{259,3},{4... | collective-permute-start | bytes 1179656 | tf_op jit(solution)/shard_map/ppermute | solution.py:35
  135.7 17.4 %all-to-all-start.5 = ((bf16[16,16,768]{2,1,0:T(8,128)(2,1)}), bf16[16,16,768]{2,1,0:T(8,128)(2,1)}, u32[]{:S(2)}, u32[]{:S(2)}) async-start(bf16[16,16,768]{2,1,0:T(8,128)(2,1)} %bitcast.117), calls=%async_computation.5 | async-start | bytes 786432 | tf_op jit(solution)/shard_map/all_to_all | solution.py:22
  139.9 2.7 %copy-start.9 = (bf16[2,8,2,16,768]{4,3,2,1,0:T(8,128)(2,1)S(1)}, bf16[2,8,2,16,768]{4,3,2,1,0:T(8,128)(2,1)}, u32[]{:S(2)}) copy-start(bf16[2,8,2,16,768]{4,3,2,1,0:T(8,128)(2,1)} %pad_maximum_fusion.1) | copy-start | bytes 2359300

commit v3 on v2

--- a/solution.py
+++ b/solution.py
@@ -67,46 +67,44 @@
         sums = pre_and_back(whole_in, whole_grad, xl) + got.astype(f32)
         return sums.astype(bf16).reshape(2, 8, tokens, hidden)
 
-    def row_sums(pairs):
-        pieces = swap(jnp.swapaxes(pairs, 0, 1).reshape(-1, hidden), "y")
-        return jnp.sum(pieces.reshape(8, 2, tokens, hidden).astype(f32), axis=0)
-
-    near = spread(jnp.concatenate([inputs, grad_out], axis=0), "z", 8)
+    both = jnp.stack([inputs, grad_out])
+    near = swap(jnp.broadcast_to(both[None], (8,) + both.shape).reshape(-1, width), "z")
     far = other(near, "xh")
     near_in, near_grad = over_cores(near)
-    near_sums = row_sums(pair_sums(near_in, near_grad))
     far_in, far_grad = over_cores(far)
-    far_sums = row_sums(pair_sums(far_in, far_grad))
+    near_pairs = pair_sums(near_in, near_grad)
+    far_pairs = pair_sums(far_in, far_grad)
+    pairs = jnp.stack([near_pairs, far_pairs], axis=1).transpose(2, 0, 1, 3, 4)
+    pieces = swap(pairs.reshape(-1, hidden), "y").reshape(8, 2, 2 * tokens, hidden)
+    pre, back = jnp.sum(pieces.astype(f32), axis=0)
 
-    pre = jnp.concatenate([near_sums[0], far_sums[0]], axis=0)
-    back = jnp.concatenate([near_sums[1], far_sums[1]], axis=0)
     gelu_value, gelu_slope = gelu_parts(pre)
-    dpre_mine = spread((back * gelu_slope).astype(bf16), "y", 8)
-    dpre_mine, act_rows = lax.optimization_barrier((dpre_mine, gelu_value.astype(bf16)))
-    dpre_other = other(dpre_mine, "xl")
+    dpre = spread((back * gelu_slope).astype(bf16), ("xl", "y"), 16)
+    dpre, act_rows = lax.optimization_barrier((dpre, gelu_value.astype(bf16)))
     act_mine = spread(act_rows, "y", 8)
 
-    def in_of(rows):
+    def in_of(which):
+        rows = half(dpre, which).reshape(8, 2, tokens, hidden)
+        rows = jnp.where(xh == 0, rows, rows[:, ::-1])
         return lax.dot_general(
-            rows, w_up, (((1,), (1,)), ((), ())), preferred_element_type=f32
+            jnp.swapaxes(rows, 0, 1).reshape(-1, hidden),
+            w_up,
+            (((1,), (1,)), ((), ())),
+            preferred_element_type=f32,
         )
 
-    from_mine, from_other = in_of(dpre_mine), in_of(dpre_other)
-    same = core == xl
-    kept = jnp.where(same, from_mine, from_other)
-    given = jnp.where(same, from_other, from_mine)
-    given, act_mine = lax.optimization_barrier((given, act_mine))
-    act_other = other(act_mine, "xl")
-    kept = (kept + other(given, "c")).astype(bf16).reshape(8, 2, tokens, width)
-    first = xh == 0
-    kept = jnp.stack(
-        [
-            jnp.where(first, kept[:, 0], kept[:, 1]),
-            jnp.where(first, kept[:, 1], kept[:, 0]),
-        ]
-    ).reshape(-1, width)
+    def got_from(given):
+        both = gather(given, "c")
+        return half(both, 1 - core)
+
+    given, kept = in_of(1 - core), in_of(core)
+    size = given.shape[0] // 2
+    got = jnp.concatenate([got_from(given[:size]), got_from(given[size:])])
+    kept = (kept + got).astype(bf16)
+    kept, act_mine = lax.optimization_barrier((kept, act_mine))
     pieces = swap(kept, ("xh", "z")).reshape(16, tokens, width)
     grad_in = jnp.sum(pieces.astype(f32), axis=0).astype(bf16)
+    act_other = other(act_mine, "xl")
 
     def by_half(near, far):
         rows = [x.reshape(2, 8, tokens, width) for x in (near, far)]
@@ -121,9 +119,12 @@
             left, right, (((0,), (0,)), ((), ())), preferred_element_type=f32
         )
 
-    in_mine, in_other = by_half(near_in, far_in)
+    def rows_of(near, far):
+        parts = [x.reshape(16, tokens, width) for x in (near, far)]
+        return jnp.stack(parts, axis=1).reshape(-1, width)
+
     grad_mine, grad_other = by_half(near_grad, far_grad)
-    grad_up = over_tokens(in_mine, dpre_mine) + over_tokens(in_other, dpre_other)
+    grad_up = over_tokens(rows_of(near_in, far_in), dpre)
     grad_down = over_tokens(act_mine, grad_mine) + over_tokens(act_other, grad_other)
     return (grad_in, grad_up.astype(bf16), grad_down.astype(bf16))
 

time: 156 us -> 152 us (0.974)
  the two profiles are of different devices: /device:TPU:1 before, /device:TPU:4 now
where the time goes in v3:
time: 152 us; the launch traced here: 151 us
  waiting for transfers between devices  58.1 us (38%)
  blocking collectives  39 us (26%)
  starting transfers between devices  35.4 us (23%)
  matrix products  10.1 us (7%)
  other arithmetic  4.72 us (3%)
  local copies, waits for them, and re-layouts  2.95 us (2%)
    all_to_all x4, waiting for transfers between devices, swap(): return lax.all_to_all(blocks, axes, split_axis=0, concat_axis=0, tiled=True)  37.6 us
    all_to_all x1, blocking collectives, swap(): return lax.all_to_all(blocks, axes, split_axis=0, concat_axis=0, tiled=True)  29.5 us
    all_to_all x4, starting transfers between devices, swap(): return lax.all_to_all(blocks, axes, split_axis=0, concat_axis=0, tiled=True)  22.9 us
    ppermute x4, waiting for transfers between devices, other(): return lax.ppermute(block, axis, [(0, 1), (1, 0)])  20.5 us
    ppermute x4, starting transfers between devices, other(): return lax.ppermute(block, axis, [(0, 1), (1, 0)])  12.6 us
    all_gather x4, blocking collectives, gather(): return lax.all_gather(block, axis, axis=0, tiled=True)  9.46 us
    dot_general x3, matrix products, over_tokens(): lax.dot_general(left, right, (((0,), (0,)), ((), ())), preferred_element_...  4.87 us
  transfers between devices with their start and end apart: 8, of which 6 were waited for; matrix products, arithmetic and copies ran while one was open for 8% of the time, Pallas kernels for 0%

profile of v3, /device:TPU:4, one launch (start us, length us, event | category | flops | bytes accessed | tf_op | source)
XLA Modules:
  0.0 151.2 jit_solution(10006282991291211079)
XLA Ops:
  0.6 0.9 pad_maximum_fusion.5
  1.5 0.8 broadcast_in_dim.9
  2.3 10.3 %all-to-all-start = ((bf16[8,32,768]{2,1,0:T(8,128)(2,1)}), bf16[8,32,768]{2,1,0:T(8,128)(2,1)S(1)}, u32[]{:S(2)}, u32[]{:S(2)}) async-start(bf16[8,32,768]{2,1,0:T(8,128)(2,1)} %broadcast_in_dim.9), calls=%async_computation | async-start | bytes 786432 | tf_op jit(solution)/shard_map/all_to_all | solution.py:22
  12.6 14.7 %all-to-all-done = bf16[8,32,768]{2,1,0:T(8,128)(2,1)S(1)} async-done(((bf16[8,32,768]{2,1,0:T(8,128)(2,1)}), bf16[8,32,768]{2,1,0:T(8,128)(2,1)S(1)}, u32[]{:S(2)}, u32[]{:S(2)}) %all-to-all-start) | async-done | bytes 393248 | tf_op jit(solution)/shard_map/all_to_all | solution.py:22
  27.3 2.5 %collective-permute-start.1 = (bf16[256,768]{1,0:T(8,128)(2,1)S(1)}, bf16[256,768]{1,0:T(8,128)(2,1)S(1)}, u32[]{:S(2)}, u32[]{:S(2)}) collective-permute-start(bf16[256,768]{1,0:T(8,128)(2,1)S(1)} %bitcast.90), channel_id=1, source_target_pairs={{0,2},{2,0},{1,3},{3,1},{4,6},{6,4},{5,7},{7,5},{8,10},{10,8},{9,1... | collective-permute-start | bytes 1179656 | tf_op jit(solution)/shard_map/ppermute | solution.py:35
  29.8 2.4 %all_gather.12 = bf16[512,768]{1,0:T(8,128)(2,1)S(1)} all-gather(bf16[256,768]{1,0:T(8,128)(2,1)S(1)} %bitcast.91), channel_id=1, replica_groups=mesh['xl'=2,'y'=8,'z'=8,'xh'=2,'c'=2] {'c'}, dimensions={0}, use_global_device_ids=true | all-gather | bytes 1179648 | tf_op jit(solution)/shard_map/all_gather | solution.py:31
  32.3 0.5 fusion.2
  32.8 0.3 fusion.1
  33.2 4.0 %collective-permute-start = (bf16[2,128,768]{2,1,0:T(8,128)(2,1)S(1)}, bf16[2,128,768]{2,1,0:T(8,128)(2,1)S(1)}, u32[]{:S(2)}, u32[]{:S(2)}) collective-permute-start(bf16[2,128,768]{2,1,0:T(8,128)(2,1)S(1)} %pad_maximum_fusion.3), channel_id=1, source_target_pairs={{0,256},{256,0},{1,257},{257,1},{2,258},{258,2},{3,259},{259,3},{4... | collective-permute-start | bytes 1179656 | tf_op jit(solution)/shard_map/ppermute | solution.py:35
  37.2 0.5 convolution_bitcast_fusion.2
  37.7 0.3 convolution_bitcast_fusion.3
  38.1 4.2 %collective-permute-done.1 = bf16[256,768]{1,0:T(8,128)(2,1)S(1)} collective-permute-done((bf16[256,768]{1,0:T(8,128)(2,1)S(1)}, bf16[256,768]{1,0:T(8,128)(2,1)S(1)}, u32[]{:S(2)}, u32[]{:S(2)}) %collective-permute-start.1) | collective-permute-done | bytes 393248 | tf_op jit(solution)/shard_map/ppermute | solution.py:35
  42.3 2.4 %all_gather.13 = bf16[512,768]{1,0:T(8,128)(2,1)S(1)} all-gather(bf16[256,768]{1,0:T(8,128)(2,1)S(1)} %collective-permute-done.1), channel_id=1, replica_groups=mesh['xl'=2,'y'=8,'z'=8,'xh'=2,'c'=2] {'c'}, dimensions={0}, use_global_device_ids=true | all-gather | bytes 1179648 | tf_op jit(solution)/shard_map/all_gather | solution.py:31
  44.7 0.5 fusion.4
  45.3 0.3 fusion.3
  45.6 2.3 %collective-permute-start.2 = (bf16[2,128,768]{2,1,0:T(8,128)(2,1)S(1)}, bf16[2,128,768]{2,1,0:T(8,128)(2,1)S(1)}, u32[]{:S(2)}, u32[]{:S(2)}) collective-permute-start(bf16[2,128,768]{2,1,0:T(8,128)(2,1)S(1)} %pad_maximum_fusion.4), channel_id=1, source_target_pairs={{0,256},{256,0},{1,257},{257,1},{2,258},{258,2},{3,259},{259,3},{4... | collective-permute-start | bytes 1179656 | tf_op jit(solution)/shard_map/ppermute | solution.py:35
  47.9 0.5 convolution_bitcast_fusion
  48.5 0.3 convolution_bitcast_fusion.1
  48.8 0.1 fusion.5
  48.9 9.8 %collective-permute-done.2 = bf16[2,128,768]{2,1,0:T(8,128)(2,1)S(1)} collective-permute-done((bf16[2,128,768]{2,1,0:T(8,128)(2,1)S(1)}, bf16[2,128,768]{2,1,0:T(8,128)(2,1)S(1)}, u32[]{:S(2)}, u32[]{:S(2)}) %collective-permute-start.2) | collective-permute-done | bytes 393248 | tf_op jit(solution)/shard_map/ppermute | solution.py:35
  58.7 0.1 fusion.6
  58.8 0.1 pad_maximum_fusion
  58.8 0.1 copy.15
  58.9 29.5 %all_to_all.45 = bf16[8,64,768]{2,1,0:T(8,128)(2,1)S(1)} all-to-all(bf16[8,64,768]{2,1,0:T(8,128)(2,1)S(1)} %bitcast.84), channel_id=1, replica_groups=mesh['xl'=2,'y'=8,'z'=8,'xh'=2,'c'=2] {'y'}, dimensions={0} | all-to-all | bytes 1572864 | tf_op jit(solution)/shard_map/all_to_all | solution.py:22
  88.4 0.1 convert_reduce_fusion
  88.5 0.7 multiply_convert_fusion
  89.2 1.0 broadcast_in_dim.10
  90.2 3.6 %all-to-all-start.2 = ((bf16[16,32,768]{2,1,0:T(8,128)(2,1)}), bf16[16,32,768]{2,1,0:T(8,128)(2,1)S(1)}, u32[]{:S(2)}, u32[]{:S(2)}) async-start(bf16[16,32,768]{2,1,0:T(8,128)(2,1)} %broadcast_in_dim.10), calls=%async_computation.2 | async-start | bytes 1572864 | tf_op jit(solution)/shard_map/all_to_all | solution.py:22
  93.8 1.0 pad_maximum_fusion.1
  94.8 1.0 pad_maximum_fusion.2
  95.8 17.4 %all-to-all-done.2 = bf16[16,32,768]{2,1,0:T(8,128)(2,1)S(1)} async-done(((bf16[16,32,768]{2,1,0:T(8,128)(2,1)}), bf16[16,32,768]{2,1,0:T(8,128)(2,1)S(1)}, u32[]{:S(2)}, u32[]{:S(2)}) %all-to-all-start.2) | async-done | bytes 786464 | tf_op jit(solution)/shard_map/all_to_all | solution.py:22
  113.1 0.8 broadcast_in_dim.11
  113.9 4.1 %all-to-all-start.3 = ((bf16[8,32,768]{2,1,0:T(8,128)(2,1)}), bf16[8,32,768]{2,1,0:T(8,128)(2,1)}, u32[]{:S(2)}, u32[]{:S(2)}) async-start(bf16[8,32,768]{2,1,0:T(8,128)(2,1)} %broadcast_in_dim.11), calls=%async_computation.3 | async-start | bytes 786432 | tf_op jit(solution)/shard_map/all_to_all | solution.py:22
  118.0 0.1 constant_dynamic-slice_fusion.2
  118.1 0.2 fusion.7
  118.3 0.5 fusion.42
  118.8 0.1 fusion.39
  118.9 2.4 %all_gather.14 = f32[256,768]{1,0:T(8,128)S(1)} all-gather(f32[128,768]{1,0:T(8,128)S(1)} %get-tuple-element.11), channel_id=1, replica_groups=mesh['xl'=2,'y'=8,'z'=8,'xh'=2,'c'=2] {'c'}, dimensions={0}, use_global_device_ids=true | all-gather | bytes 1179648 | tf_op jit(solution)/shard_map/all_gather | solution.py:31
  121.3 2.4 %all_gather.15 = f32[256,768]{1,0:T(8,128)S(1)} all-gather(f32[128,768]{1,0:T(8,128)S(1)} %get-tuple-element.12), channel_id=1, replica_groups=mesh['xl'=2,'y'=8,'z'=8,'xh'=2,'c'=2] {'c'}, dimensions={0}, use_global_device_ids=true | all-gather | bytes 1179648 | tf_op jit(solution)/shard_map/all_gather | solution.py:31
  123.7 1.3 fusion
  125.0 5.6 %all-to-all-done.3 = bf16[8,32,768]{2,1,0:T(8,128)(2,1)} async-done(((bf16[8,32,768]{2,1,0:T(8,128)(2,1)}), bf16[8,32,768]{2,1,0:T(8,128)(2,1)}, u32[]{:S(2)}, u32[]{:S(2)}) %all-to-all-start.3) | async-done | bytes 393248 | tf_op jit(solution)/shard_map/all_to_all | solution.py:22
  130.5 4.8 %all-to-all-start.4 = ((bf16[16,16,768]{2,1,0:T(8,128)(2,1)}), bf16[16,16,768]{2,1,0:T(8,128)(2,1)S(1)}, u32[]{:S(2)}, u32[]{:S(2)}) async-start(bf16[16,16,768]{2,1,0:T(8,128)(2,1)} %bitcast.30), calls=%async_computation.4 | async-start | bytes 786432 | tf_op jit(solution)/shard_map/all_to_all | solution.py:22
  135.4 3.8 %collective-permute-start.3 = (bf16[256,768]{1,0:T(8,128)(2,1)}, bf16[256,768]{1,0:T(8,128)(2,1)S(1)}, u32[]{:S(2)}, u32[]{:S(2)}) collective-permute-start(bf16[256,768]{1,0:T(8,128)(2,1)} %bitcast.29), channel_id=1, source_target_pairs={{0,256},{256,0},{1,257},{257,1},{2,258},{258,2},{3,259},{259,3},{4... | collective-permute-start | bytes 1179656 | tf_op jit(solution)/shard_map/ppermute | solution.py:35
  139.2 1.8 %convolution_convert_fusion = bf16[768,768]{1,0:T(8,128)(2,1)} fusion(bf16[512,768]{1,0:T(8,128)(2,1)S(1)} %bitcast.97, bf16[512,768]{1,0:T(8,128)(2,1)S(1)} %bitcast.86), kind=kOutput, calls=%fused_computation.2 | convolution fusion | flops 604569600 | bytes 2752512 | tf_op jit(solution)/shard_map/dot_general | solution.py:118
  141.0 1.5 %fusion.10 = f32[768,768]{1,0:T(8,128)S(1)} fusion(bf16[256,768]{1,0:T(8,128)(2,1)} %bitcast.29, bf16[2,256,768]{2,1,0:T(8,128)(2,1)S(1)} %bitcast.87, s32[]{:T(128)S(6)} %select_n.49), kind=kOutput, calls=%fused_computation.31 | convolution fusion | flops 301989888 | bytes 3145732 | tf_op jit(solution)/shard_map/dot_general | solution.py:118
  142.5 6.5 %collective-permute-done.3 = bf16[256,768]{1,0:T(8,128)(2,1)S(1)} collective-permute-done((bf16[256,768]{1,0:T(8,128)(2,1)}, bf16[256,768]{1,0:T(8,128)(2,1)S(1)}, u32[]{:S(2)}, u32[]{:S(2)}) %collective-permute-start.3) | collective-permute-done | bytes 393248 | tf_op jit(solution)/shard_map/ppermute | solution.py:35
  149.0 1.5 %add_convert_fusion = bf16[768,768]{1,0:T(8,128)(2,1)} fusion(f32[768,768]{1,0:T(8,128)S(1)} %fusion.10, bf16[256,768]{1,0:T(8,128)(2,1)S(1)} %collective-permute-done.3, bf16[2,256,768]{2,1,0:T(8,128)(2,1)S(1)} %bitcast.88, s32[]{:T(128)S(6)} %select_n.50), kind=kOutput, calls=%fused_computation | convolution fusion | flops 303169536 | bytes 4325380 | tf_op jit(solution)/shard_map/dot_general | solution.py:118
  150.5 0.7 reduce_sum.22
  (20 shorter events, 0.3 us)
Async XLA Ops:
  0.6 32.2 %copy-start = (bf16[768,768]{1,0:T(8,128)(2,1)S(1)}, bf16[768,768]{1,0:T(8,128)(2,1)}, u32[]{:S(2)}) copy-start(bf16[768,768]{1,0:T(8,128)(2,1)} %param.5) | copy-start | bytes 3538948
  2.3 25.0 %all-to-all-start = ((bf16[8,32,768]{2,1,0:T(8,128)(2,1)}), bf16[8,32,768]{2,1,0:T(8,128)(2,1)S(1)}, u32[]{:S(2)}, u32[]{:S(2)}) async-start(bf16[8,32,768]{2,1,0:T(8,128)(2,1)} %broadcast_in_dim.9), calls=%async_computation | async-start | bytes 786432 | tf_op jit(solution)/shard_map/all_to_all | solution.py:22
  27.3 5.0 %copy-start.1 = (bf16[768,768]{1,0:T(8,128)(2,1)S(1)}, bf16[768,768]{1,0:T(8,128)(2,1)}, u32[]{:S(2)}) copy-start(bf16[768,768]{1,0:T(8,128)(2,1)} %param.6) | copy-start | bytes 3538948
  27.3 15.0 %collective-permute-start.1 = (bf16[256,768]{1,0:T(8,128)(2,1)S(1)}, bf16[256,768]{1,0:T(8,128)(2,1)S(1)}, u32[]{:S(2)}, u32[]{:S(2)}) collective-permute-start(bf16[256,768]{1,0:T(8,128)(2,1)S(1)} %bitcast.90), channel_id=1, source_target_pairs={{0,2},{2,0},{1,3},{3,1},{4,6},{6,4},{5,7},{7,5},{8,10},{10,8},{9,1... | collective-permute-start | bytes 1179656 | tf_op jit(solution)/shard_map/ppermute | solution.py:35
  33.2 15.6 %collective-permute-start = (bf16[2,128,768]{2,1,0:T(8,128)(2,1)S(1)}, bf16[2,128,768]{2,1,0:T(8,128)(2,1)S(1)}, u32[]{:S(2)}, u32[]{:S(2)}) collective-permute-start(bf16[2,128,768]{2,1,0:T(8,128)(2,1)S(1)} %pad_maximum_fusion.3), channel_id=1, source_target_pairs={{0,256},{256,0},{1,257},{257,1},{2,258},{258,2},{3,259},{259,3},{4... | collective-permute-start | bytes 1179656 | tf_op jit(solution)/shard_map/ppermute | solution.py:35
  45.6 13.0 %collective-permute-start.2 = (bf16[2,128,768]{2,1,0:T(8,128)(2,1)S(1)}, bf16[2,128,768]{2,1,0:T(8,128)(2,1)S(1)}, u32[]{:S(2)}, u32[]{:S(2)}) collective-permute-start(bf16[2,128,768]{2,1,0:T(8,128)(2,1)S(1)} %pad_maximum_fusion.4), channel_id=1, source_target_pairs={{0,256},{256,0},{1,257},{257,1},{2,258},{258,2},{3,259},{259,3},{4... | collective-permute-start | bytes 1179656 | tf_op jit(solution)/shard_map/ppermute | solution.py:35
  90.2 22.9 %all-to-all-start.2 = ((bf16[16,32,768]{2,1,0:T(8,128)(2,1)}), bf16[16,32,768]{2,1,0:T(8,128)(2,1)S(1)}, u32[]{:S(2)}, u32[]{:S(2)}) async-start(bf16[16,32,768]{2,1,0:T(8,128)(2,1)} %broadcast_in_dim.10), calls=%async_computation.2 | async-start | bytes 1572864 | tf_op jit(solution)/shard_map/all_to_all | solution.py:22
  94.8 18.3 %copy-start.4 = (bf16[32,768]{1,0:T(8,128)(2,1)S(1)}, bf16[32,768]{1,0:T(8,128)(2,1)}, u32[]{:S(2)}) copy-start(bf16[32,768]{1,0:T(8,128)(2,1)} %get-tuple-element.8) | copy-start | bytes 147460
  113.9 16.7 %all-to-all-start.3 = ((bf16[8,32,768]{2,1,0:T(8,128)(2,1)}), bf16[8,32,768]{2,1,0:T(8,128)(2,1)}, u32[]{:S(2)}, u32[]{:S(2)}) async-start(bf16[8,32,768]{2,1,0:T(8,128)(2,1)} %broadcast_in_dim.11), calls=%async_computation.3 | async-start | bytes 786432 | tf_op jit(solution)/shard_map/all_to_all | solution.py:22
  123.7 15.5 %copy-start.3 = (bf16[16,2,16,768]{3,2,1,0:T(8,128)(2,1)S(1)}, bf16[16,2,16,768]{3,2,1,0:T(8,128)(2,1)}, u32[]{:S(2)}) copy-start(bf16[16,2,16,768]{3,2,1,0:T(8,128)(2,1)} %pad_maximum_fusion.1) | copy-start | bytes 2359300
  130.5 20.0 %all-to-all-start.4 = ((bf16[16,16,768]{2,1,0:T(8,128)(2,1)}), bf16[16,16,768]{2,1,0:T(8,128)(2,1)S(1)}, u32[]{:S(2)}, u32[]{:S(2)}) async-start(bf16[16,16,768]{2,1,0:T(8,128)(2,1)} %bitcast.30), calls=%async_computation.4 | async-start | bytes 786432 | tf_op jit(solution)/shard_map/all_to_all | solution.py:22
  135.4 13.6 %collective-permute-start.3 = (bf16[256,768]{1,0:T(8,128)(2,1)}, bf16[256,768]{1,0:T(8,128)(2,1)S(1)}, u32[]{:S(2)}, u32[]{:S(2)}) collective-permute-start(bf16[256,768]{1,0:T(8,128)(2,1)} %bitcast.29), channel_id=1, source_target_pairs={{0,256},{256,0},{1,257},{257,1},{2,258},{258,2},{3,259},{259,3},{4... | collective-permute-start | bytes 1179656 | tf_op jit(solution)/shard_map/ppermute | solution.py:35
  139.2 1.8 %copy-start.2 = (bf16[2,8,2,16,768]{4,3,2,1,0:T(8,128)(2,1)S(1)}, bf16[2,8,2,16,768]{4,3,2,1,0:T(8,128)(2,1)}, u32[]{:S(2)}) copy-start(bf16[2,8,2,16,768]{4,3,2,1,0:T(8,128)(2,1)} %pad_maximum_fusion.2) | copy-start | bytes 2359300

commit v4 on v3

--- a/solution.py
+++ b/solution.py
@@ -82,6 +82,7 @@
     dpre = spread((back * gelu_slope).astype(bf16), ("xl", "y"), 16)
     dpre, act_rows = lax.optimization_barrier((dpre, gelu_value.astype(bf16)))
     act_mine = spread(act_rows, "y", 8)
+    act_other = other(act_mine, "xl")
 
     def in_of(which):
         rows = half(dpre, which).reshape(8, 2, tokens, hidden)
@@ -104,8 +105,6 @@
     kept, act_mine = lax.optimization_barrier((kept, act_mine))
     pieces = swap(kept, ("xh", "z")).reshape(16, tokens, width)
     grad_in = jnp.sum(pieces.astype(f32), axis=0).astype(bf16)
-    act_other = other(act_mine, "xl")
-
     def by_half(near, far):
         rows = [x.reshape(2, 8, tokens, width) for x in (near, far)]
         rows = jnp.stack(rows, axis=2).reshape(2, -1, width)

time: 152 us -> 151 us (level)
  the two profiles are of different devices: /device:TPU:4 before, /device:TPU:64 now
where the time goes in v4:
time: 151 us; the launch traced here: 150 us
  waiting for transfers between devices  53.2 us (35%)
  starting transfers between devices  39 us (26%)
  blocking collectives  39 us (26%)
  matrix products  10.1 us (7%)
  other arithmetic  4.72 us (3%)
  local copies, waits for them, and re-layouts  2.95 us (2%)
    all_to_all x4, waiting for transfers between devices, swap(): return lax.all_to_all(blocks, axes, split_axis=0, concat_axis=0, tiled=True)  42.8 us
    all_to_all x1, blocking collectives, swap(): return lax.all_to_all(blocks, axes, split_axis=0, concat_axis=0, tiled=True)  29.5 us
    all_to_all x4, starting transfers between devices, swap(): return lax.all_to_all(blocks, axes, split_axis=0, concat_axis=0, tiled=True)  25 us
    ppermute x4, starting transfers between devices, other(): return lax.ppermute(block, axis, [(0, 1), (1, 0)])  14 us
    ppermute x4, waiting for transfers between devices, other(): return lax.ppermute(block, axis, [(0, 1), (1, 0)])  10.4 us
    all_gather x4, blocking collectives, gather(): return lax.all_gather(block, axis, axis=0, tiled=True)  9.48 us
    dot_general x3, matrix products, over_tokens(): lax.dot_general(left, right, (((0,), (0,)), ((), ())), preferred_element_...  4.88 us
  transfers between devices with their start and end apart: 8, of which 6 were waited for; matrix products, arithmetic and copies ran while one was open for 8% of the time, Pallas kernels for 0%

profile of v4, /device:TPU:64, one launch (start us, length us, event | category | flops | bytes accessed | tf_op | source)
XLA Modules:
  0.0 149.9 jit_solution(13148673475476023481)
XLA Ops:
  0.6 0.9 pad_maximum_fusion.5
  1.5 0.8 broadcast_in_dim.9
  2.3 10.0 %all-to-all-start = ((bf16[8,32,768]{2,1,0:T(8,128)(2,1)}), bf16[8,32,768]{2,1,0:T(8,128)(2,1)S(1)}, u32[]{:S(2)}, u32[]{:S(2)}) async-start(bf16[8,32,768]{2,1,0:T(8,128)(2,1)} %broadcast_in_dim.9), calls=%async_computation | async-start | bytes 786432 | tf_op jit(solution)/shard_map/all_to_all | solution.py:22
  12.2 13.2 %all-to-all-done = bf16[8,32,768]{2,1,0:T(8,128)(2,1)S(1)} async-done(((bf16[8,32,768]{2,1,0:T(8,128)(2,1)}), bf16[8,32,768]{2,1,0:T(8,128)(2,1)S(1)}, u32[]{:S(2)}, u32[]{:S(2)}) %all-to-all-start) | async-done | bytes 393248 | tf_op jit(solution)/shard_map/all_to_all | solution.py:22
  25.5 5.1 %collective-permute-start.1 = (bf16[256,768]{1,0:T(8,128)(2,1)S(1)}, bf16[256,768]{1,0:T(8,128)(2,1)S(1)}, u32[]{:S(2)}, u32[]{:S(2)}) collective-permute-start(bf16[256,768]{1,0:T(8,128)(2,1)S(1)} %bitcast.90), channel_id=1, source_target_pairs={{0,2},{2,0},{1,3},{3,1},{4,6},{6,4},{5,7},{7,5},{8,10},{10,8},{9,1... | collective-permute-start | bytes 1179656 | tf_op jit(solution)/shard_map/ppermute | solution.py:35
  30.5 2.4 %all_gather.12 = bf16[512,768]{1,0:T(8,128)(2,1)S(1)} all-gather(bf16[256,768]{1,0:T(8,128)(2,1)S(1)} %bitcast.91), channel_id=1, replica_groups=mesh['xl'=2,'y'=8,'z'=8,'xh'=2,'c'=2] {'c'}, dimensions={0}, use_global_device_ids=true | all-gather | bytes 1179648 | tf_op jit(solution)/shard_map/all_gather | solution.py:31
  33.0 0.5 fusion.2
  33.5 0.3 fusion.1
  33.9 2.5 %collective-permute-start = (bf16[2,128,768]{2,1,0:T(8,128)(2,1)S(1)}, bf16[2,128,768]{2,1,0:T(8,128)(2,1)S(1)}, u32[]{:S(2)}, u32[]{:S(2)}) collective-permute-start(bf16[2,128,768]{2,1,0:T(8,128)(2,1)S(1)} %pad_maximum_fusion.3), channel_id=1, source_target_pairs={{0,256},{256,0},{1,257},{257,1},{2,258},{258,2},{3,259},{259,3},{4... | collective-permute-start | bytes 1179656 | tf_op jit(solution)/shard_map/ppermute | solution.py:35
  36.4 0.5 convolution_bitcast_fusion.2
  37.0 0.3 convolution_bitcast_fusion.3
  37.3 2.4 %all_gather.13 = bf16[512,768]{1,0:T(8,128)(2,1)S(1)} all-gather(bf16[256,768]{1,0:T(8,128)(2,1)S(1)} %collective-permute-done.1), channel_id=1, replica_groups=mesh['xl'=2,'y'=8,'z'=8,'xh'=2,'c'=2] {'c'}, dimensions={0}, use_global_device_ids=true | all-gather | bytes 1179648 | tf_op jit(solution)/shard_map/all_gather | solution.py:31
  39.7 0.5 fusion.4
  40.3 0.3 fusion.3
  40.7 3.3 %collective-permute-start.2 = (bf16[2,128,768]{2,1,0:T(8,128)(2,1)S(1)}, bf16[2,128,768]{2,1,0:T(8,128)(2,1)S(1)}, u32[]{:S(2)}, u32[]{:S(2)}) collective-permute-start(bf16[2,128,768]{2,1,0:T(8,128)(2,1)S(1)} %pad_maximum_fusion.4), channel_id=1, source_target_pairs={{0,256},{256,0},{1,257},{257,1},{2,258},{258,2},{3,259},{259,3},{4... | collective-permute-start | bytes 1179656 | tf_op jit(solution)/shard_map/ppermute | solution.py:35
  44.0 0.5 convolution_bitcast_fusion
  44.6 0.3 convolution_bitcast_fusion.1
  44.9 2.9 %collective-permute-done = bf16[2,128,768]{2,1,0:T(8,128)(2,1)S(1)} collective-permute-done((bf16[2,128,768]{2,1,0:T(8,128)(2,1)S(1)}, bf16[2,128,768]{2,1,0:T(8,128)(2,1)S(1)}, u32[]{:S(2)}, u32[]{:S(2)}) %collective-permute-start) | collective-permute-done | bytes 393248 | tf_op jit(solution)/shard_map/ppermute | solution.py:35
  47.8 0.1 fusion.5
  47.8 7.5 %collective-permute-done.2 = bf16[2,128,768]{2,1,0:T(8,128)(2,1)S(1)} collective-permute-done((bf16[2,128,768]{2,1,0:T(8,128)(2,1)S(1)}, bf16[2,128,768]{2,1,0:T(8,128)(2,1)S(1)}, u32[]{:S(2)}, u32[]{:S(2)}) %collective-permute-start.2) | collective-permute-done | bytes 393248 | tf_op jit(solution)/shard_map/ppermute | solution.py:35
  55.4 0.1 fusion.6
  55.5 0.1 pad_maximum_fusion
  55.5 0.1 copy.15
  55.6 29.5 %all_to_all.45 = bf16[8,64,768]{2,1,0:T(8,128)(2,1)S(1)} all-to-all(bf16[8,64,768]{2,1,0:T(8,128)(2,1)S(1)} %bitcast.84), channel_id=1, replica_groups=mesh['xl'=2,'y'=8,'z'=8,'xh'=2,'c'=2] {'y'}, dimensions={0} | all-to-all | bytes 1572864 | tf_op jit(solution)/shard_map/all_to_all | solution.py:22
  85.1 0.1 convert_reduce_fusion
  85.2 0.7 multiply_convert_fusion
  85.9 1.0 broadcast_in_dim.10
  86.9 3.6 %all-to-all-start.2 = ((bf16[16,32,768]{2,1,0:T(8,128)(2,1)}), bf16[16,32,768]{2,1,0:T(8,128)(2,1)S(1)}, u32[]{:S(2)}, u32[]{:S(2)}) async-start(bf16[16,32,768]{2,1,0:T(8,128)(2,1)} %broadcast_in_dim.10), calls=%async_computation.2 | async-start | bytes 1572864 | tf_op jit(solution)/shard_map/all_to_all | solution.py:22
  90.5 1.0 pad_maximum_fusion.1
  91.5 1.0 pad_maximum_fusion.2
  92.4 17.4 %all-to-all-done.2 = bf16[16,32,768]{2,1,0:T(8,128)(2,1)S(1)} async-done(((bf16[16,32,768]{2,1,0:T(8,128)(2,1)}), bf16[16,32,768]{2,1,0:T(8,128)(2,1)S(1)}, u32[]{:S(2)}, u32[]{:S(2)}) %all-to-all-start.2) | async-done | bytes 786464 | tf_op jit(solution)/shard_map/all_to_all | solution.py:22
  109.8 0.8 broadcast_in_dim.11
  110.6 4.1 %all-to-all-start.3 = ((bf16[8,32,768]{2,1,0:T(8,128)(2,1)}), bf16[8,32,768]{2,1,0:T(8,128)(2,1)}, u32[]{:S(2)}, u32[]{:S(2)}) async-start(bf16[8,32,768]{2,1,0:T(8,128)(2,1)} %broadcast_in_dim.11), calls=%async_computation.3 | async-start | bytes 786432 | tf_op jit(solution)/shard_map/all_to_all | solution.py:22
  114.7 0.1 constant_dynamic-slice_fusion.2
  114.8 0.2 fusion.7
  115.0 0.5 fusion.42
  115.5 0.1 fusion.39
  115.6 2.4 %all_gather.14 = f32[256,768]{1,0:T(8,128)S(1)} all-gather(f32[128,768]{1,0:T(8,128)S(1)} %get-tuple-element.11), channel_id=1, replica_groups=mesh['xl'=2,'y'=8,'z'=8,'xh'=2,'c'=2] {'c'}, dimensions={0}, use_global_device_ids=true | all-gather | bytes 1179648 | tf_op jit(solution)/shard_map/all_gather | solution.py:31
  118.0 2.4 %all_gather.15 = f32[256,768]{1,0:T(8,128)S(1)} all-gather(f32[128,768]{1,0:T(8,128)S(1)} %get-tuple-element.12), channel_id=1, replica_groups=mesh['xl'=2,'y'=8,'z'=8,'xh'=2,'c'=2] {'c'}, dimensions={0}, use_global_device_ids=true | all-gather | bytes 1179648 | tf_op jit(solution)/shard_map/all_gather | solution.py:31
  120.4 1.3 fusion
  121.7 5.6 %all-to-all-done.3 = bf16[8,32,768]{2,1,0:T(8,128)(2,1)} async-done(((bf16[8,32,768]{2,1,0:T(8,128)(2,1)}), bf16[8,32,768]{2,1,0:T(8,128)(2,1)}, u32[]{:S(2)}, u32[]{:S(2)}) %all-to-all-start.3) | async-done | bytes 393248 | tf_op jit(solution)/shard_map/all_to_all | solution.py:22
  127.2 3.1 %collective-permute-start.3 = (bf16[256,768]{1,0:T(8,128)(2,1)}, bf16[256,768]{1,0:T(8,128)(2,1)S(1)}, u32[]{:S(2)}, u32[]{:S(2)}) collective-permute-start(bf16[256,768]{1,0:T(8,128)(2,1)} %bitcast.29), channel_id=1, source_target_pairs={{0,256},{256,0},{1,257},{257,1},{2,258},{258,2},{3,259},{259,3},{4... | collective-permute-start | bytes 1179656 | tf_op jit(solution)/shard_map/ppermute | solution.py:35
  130.3 7.3 %all-to-all-start.4 = ((bf16[16,16,768]{2,1,0:T(8,128)(2,1)}), bf16[16,16,768]{2,1,0:T(8,128)(2,1)S(1)}, u32[]{:S(2)}, u32[]{:S(2)}) async-start(bf16[16,16,768]{2,1,0:T(8,128)(2,1)} %bitcast.30), calls=%async_computation.4 | async-start | bytes 786432 | tf_op jit(solution)/shard_map/all_to_all | solution.py:22
  137.7 1.8 %convolution_convert_fusion = bf16[768,768]{1,0:T(8,128)(2,1)} fusion(bf16[512,768]{1,0:T(8,128)(2,1)S(1)} %bitcast.97, bf16[512,768]{1,0:T(8,128)(2,1)S(1)} %bitcast.86), kind=kOutput, calls=%fused_computation.2 | convolution fusion | flops 604569600 | bytes 2752512 | tf_op jit(solution)/shard_map/dot_general | solution.py:117
  139.5 1.5 %fusion.10 = f32[768,768]{1,0:T(8,128)S(1)} fusion(bf16[256,768]{1,0:T(8,128)(2,1)} %bitcast.29, bf16[2,256,768]{2,1,0:T(8,128)(2,1)S(1)} %bitcast.87, s32[]{:T(128)S(6)} %select_n.49), kind=kOutput, calls=%fused_computation.31 | convolution fusion | flops 301989888 | bytes 3145732 | tf_op jit(solution)/shard_map/dot_general | solution.py:117
  141.0 1.5 %add_convert_fusion = bf16[768,768]{1,0:T(8,128)(2,1)} fusion(f32[768,768]{1,0:T(8,128)S(1)} %fusion.10, bf16[256,768]{1,0:T(8,128)(2,1)S(1)} %collective-permute-done.3, bf16[2,256,768]{2,1,0:T(8,128)(2,1)S(1)} %bitcast.88, s32[]{:T(128)S(6)} %select_n.50), kind=kOutput, calls=%fused_computation | convolution fusion | flops 303169536 | bytes 4325380 | tf_op jit(solution)/shard_map/dot_general | solution.py:117
  142.6 6.7 %all-to-all-done.4 = bf16[16,16,768]{2,1,0:T(8,128)(2,1)S(1)} async-done(((bf16[16,16,768]{2,1,0:T(8,128)(2,1)}), bf16[16,16,768]{2,1,0:T(8,128)(2,1)S(1)}, u32[]{:S(2)}, u32[]{:S(2)}) %all-to-all-start.4) | async-done | bytes 393248 | tf_op jit(solution)/shard_map/all_to_all | solution.py:22
  149.2 0.7 reduce_sum.22
  (20 shorter events, 0.3 us)
Async XLA Ops:
  0.6 32.9 %copy-start = (bf16[768,768]{1,0:T(8,128)(2,1)S(1)}, bf16[768,768]{1,0:T(8,128)(2,1)}, u32[]{:S(2)}) copy-start(bf16[768,768]{1,0:T(8,128)(2,1)} %param.5) | copy-start | bytes 3538948
  2.3 23.2 %all-to-all-start = ((bf16[8,32,768]{2,1,0:T(8,128)(2,1)}), bf16[8,32,768]{2,1,0:T(8,128)(2,1)S(1)}, u32[]{:S(2)}, u32[]{:S(2)}) async-start(bf16[8,32,768]{2,1,0:T(8,128)(2,1)} %broadcast_in_dim.9), calls=%async_computation | async-start | bytes 786432 | tf_op jit(solution)/shard_map/all_to_all | solution.py:22
  25.5 7.5 %copy-start.1 = (bf16[768,768]{1,0:T(8,128)(2,1)S(1)}, bf16[768,768]{1,0:T(8,128)(2,1)}, u32[]{:S(2)}) copy-start(bf16[768,768]{1,0:T(8,128)(2,1)} %param.6) | copy-start | bytes 3538948
  25.5 11.8 %collective-permute-start.1 = (bf16[256,768]{1,0:T(8,128)(2,1)S(1)}, bf16[256,768]{1,0:T(8,128)(2,1)S(1)}, u32[]{:S(2)}, u32[]{:S(2)}) collective-permute-start(bf16[256,768]{1,0:T(8,128)(2,1)S(1)} %bitcast.90), channel_id=1, source_target_pairs={{0,2},{2,0},{1,3},{3,1},{4,6},{6,4},{5,7},{7,5},{8,10},{10,8},{9,1... | collective-permute-start | bytes 1179656 | tf_op jit(solution)/shard_map/ppermute | solution.py:35
  33.9 13.9 %collective-permute-start = (bf16[2,128,768]{2,1,0:T(8,128)(2,1)S(1)}, bf16[2,128,768]{2,1,0:T(8,128)(2,1)S(1)}, u32[]{:S(2)}, u32[]{:S(2)}) collective-permute-start(bf16[2,128,768]{2,1,0:T(8,128)(2,1)S(1)} %pad_maximum_fusion.3), channel_id=1, source_target_pairs={{0,256},{256,0},{1,257},{257,1},{2,258},{258,2},{3,259},{259,3},{4... | collective-permute-start | bytes 1179656 | tf_op jit(solution)/shard_map/ppermute | solution.py:35
  40.7 14.7 %collective-permute-start.2 = (bf16[2,128,768]{2,1,0:T(8,128)(2,1)S(1)}, bf16[2,128,768]{2,1,0:T(8,128)(2,1)S(1)}, u32[]{:S(2)}, u32[]{:S(2)}) collective-permute-start(bf16[2,128,768]{2,1,0:T(8,128)(2,1)S(1)} %pad_maximum_fusion.4), channel_id=1, source_target_pairs={{0,256},{256,0},{1,257},{257,1},{2,258},{258,2},{3,259},{259,3},{4... | collective-permute-start | bytes 1179656 | tf_op jit(solution)/shard_map/ppermute | solution.py:35
  86.9 22.9 %all-to-all-start.2 = ((bf16[16,32,768]{2,1,0:T(8,128)(2,1)}), bf16[16,32,768]{2,1,0:T(8,128)(2,1)S(1)}, u32[]{:S(2)}, u32[]{:S(2)}) async-start(bf16[16,32,768]{2,1,0:T(8,128)(2,1)} %broadcast_in_dim.10), calls=%async_computation.2 | async-start | bytes 1572864 | tf_op jit(solution)/shard_map/all_to_all | solution.py:22
  91.5 18.3 %copy-start.4 = (bf16[32,768]{1,0:T(8,128)(2,1)S(1)}, bf16[32,768]{1,0:T(8,128)(2,1)}, u32[]{:S(2)}) copy-start(bf16[32,768]{1,0:T(8,128)(2,1)} %get-tuple-element.8) | copy-start | bytes 147460
  110.6 16.7 %all-to-all-start.3 = ((bf16[8,32,768]{2,1,0:T(8,128)(2,1)}), bf16[8,32,768]{2,1,0:T(8,128)(2,1)}, u32[]{:S(2)}, u32[]{:S(2)}) async-start(bf16[8,32,768]{2,1,0:T(8,128)(2,1)} %broadcast_in_dim.11), calls=%async_computation.3 | async-start | bytes 786432 | tf_op jit(solution)/shard_map/all_to_all | solution.py:22
  120.4 17.3 %copy-start.3 = (bf16[16,2,16,768]{3,2,1,0:T(8,128)(2,1)S(1)}, bf16[16,2,16,768]{3,2,1,0:T(8,128)(2,1)}, u32[]{:S(2)}) copy-start(bf16[16,2,16,768]{3,2,1,0:T(8,128)(2,1)} %pad_maximum_fusion.1) | copy-start | bytes 2359300
  127.2 13.8 %collective-permute-start.3 = (bf16[256,768]{1,0:T(8,128)(2,1)}, bf16[256,768]{1,0:T(8,128)(2,1)S(1)}, u32[]{:S(2)}, u32[]{:S(2)}) collective-permute-start(bf16[256,768]{1,0:T(8,128)(2,1)} %bitcast.29), channel_id=1, source_target_pairs={{0,256},{256,0},{1,257},{257,1},{2,258},{258,2},{3,259},{259,3},{4... | collective-permute-start | bytes 1179656 | tf_op jit(solution)/shard_map/ppermute | solution.py:35
  130.3 18.9 %all-to-all-start.4 = ((bf16[16,16,768]{2,1,0:T(8,128)(2,1)}), bf16[16,16,768]{2,1,0:T(8,128)(2,1)S(1)}, u32[]{:S(2)}, u32[]{:S(2)}) async-start(bf16[16,16,768]{2,1,0:T(8,128)(2,1)} %bitcast.30), calls=%async_computation.4 | async-start | bytes 786432 | tf_op jit(solution)/shard_map/all_to_all | solution.py:22
  137.7 1.8 %copy-start.2 = (bf16[2,8,2,16,768]{4,3,2,1,0:T(8,128)(2,1)S(1)}, bf16[2,8,2,16,768]{4,3,2,1,0:T(8,128)(2,1)}, u32[]{:S(2)}) copy-start(bf16[2,8,2,16,768]{4,3,2,1,0:T(8,128)(2,1)} %pad_maximum_fusion.2) | copy-start | bytes 2359300

commit v5 on v4

--- a/solution.py
+++ b/solution.py
@@ -80,8 +80,10 @@
 
     gelu_value, gelu_slope = gelu_parts(pre)
     dpre = spread((back * gelu_slope).astype(bf16), ("xl", "y"), 16)
-    dpre, act_rows = lax.optimization_barrier((dpre, gelu_value.astype(bf16)))
-    act_mine = spread(act_rows, "y", 8)
+    act_rows = gelu_value.astype(bf16)
+    act_copies = jnp.broadcast_to(act_rows[None], (8,) + act_rows.shape)
+    dpre, act_copies = lax.optimization_barrier((dpre, act_copies))
+    act_mine = swap(act_copies.reshape(-1, hidden), "y")
     act_other = other(act_mine, "xl")
 
     def in_of(which):

time: 151 us -> 151 us (level)
  no operation moved by 1% of the time
where the time goes in v5:
time: 151 us; the launch traced here: 150 us
  waiting for transfers between devices  53.2 us (35%)
  starting transfers between devices  39 us (26%)
  blocking collectives  39 us (26%)
  matrix products  10.1 us (7%)
  other arithmetic  4.72 us (3%)
  local copies, waits for them, and re-layouts  2.95 us (2%)
    all_to_all x4, waiting for transfers between devices, swap(): return lax.all_to_all(blocks, axes, split_axis=0, concat_axis=0, tiled=True)  42.8 us
    all_to_all x1, blocking collectives, swap(): return lax.all_to_all(blocks, axes, split_axis=0, concat_axis=0, tiled=True)  29.5 us
    all_to_all x4, starting transfers between devices, swap(): return lax.all_to_all(blocks, axes, split_axis=0, concat_axis=0, tiled=True)  25 us
    ppermute x4, starting transfers between devices, other(): return lax.ppermute(block, axis, [(0, 1), (1, 0)])  14 us
    ppermute x4, waiting for transfers between devices, other(): return lax.ppermute(block, axis, [(0, 1), (1, 0)])  10.4 us
    all_gather x4, blocking collectives, gather(): return lax.all_gather(block, axis, axis=0, tiled=True)  9.48 us
    dot_general x3, matrix products, over_tokens(): lax.dot_general(left, right, (((0,), (0,)), ((), ())), preferred_element_...  4.88 us
  transfers between devices with their start and end apart: 8, of which 6 were waited for; matrix products, arithmetic and copies ran while one was open for 8% of the time, Pallas kernels for 0%

profile of v5, /device:TPU:64, one launch (start us, length us, event | category | flops | bytes accessed | tf_op | source)
XLA Modules:
  0.0 149.9 jit_solution(13148673475476023481)
XLA Ops:
  0.6 0.9 pad_maximum_fusion.5
  1.5 0.8 broadcast_in_dim.9
  2.3 10.0 %all-to-all-start = ((bf16[8,32,768]{2,1,0:T(8,128)(2,1)}), bf16[8,32,768]{2,1,0:T(8,128)(2,1)S(1)}, u32[]{:S(2)}, u32[]{:S(2)}) async-start(bf16[8,32,768]{2,1,0:T(8,128)(2,1)} %broadcast_in_dim.9), calls=%async_computation | async-start | bytes 786432 | tf_op jit(solution)/shard_map/all_to_all | solution.py:22
  12.2 13.2 %all-to-all-done = bf16[8,32,768]{2,1,0:T(8,128)(2,1)S(1)} async-done(((bf16[8,32,768]{2,1,0:T(8,128)(2,1)}), bf16[8,32,768]{2,1,0:T(8,128)(2,1)S(1)}, u32[]{:S(2)}, u32[]{:S(2)}) %all-to-all-start) | async-done | bytes 393248 | tf_op jit(solution)/shard_map/all_to_all | solution.py:22
  25.5 5.1 %collective-permute-start.1 = (bf16[256,768]{1,0:T(8,128)(2,1)S(1)}, bf16[256,768]{1,0:T(8,128)(2,1)S(1)}, u32[]{:S(2)}, u32[]{:S(2)}) collective-permute-start(bf16[256,768]{1,0:T(8,128)(2,1)S(1)} %bitcast.90), channel_id=1, source_target_pairs={{0,2},{2,0},{1,3},{3,1},{4,6},{6,4},{5,7},{7,5},{8,10},{10,8},{9,1... | collective-permute-start | bytes 1179656 | tf_op jit(solution)/shard_map/ppermute | solution.py:35
  30.5 2.4 %all_gather.12 = bf16[512,768]{1,0:T(8,128)(2,1)S(1)} all-gather(bf16[256,768]{1,0:T(8,128)(2,1)S(1)} %bitcast.91), channel_id=1, replica_groups=mesh['xl'=2,'y'=8,'z'=8,'xh'=2,'c'=2] {'c'}, dimensions={0}, use_global_device_ids=true | all-gather | bytes 1179648 | tf_op jit(solution)/shard_map/all_gather | solution.py:31
  33.0 0.5 fusion.2
  33.5 0.3 fusion.1
  33.9 2.5 %collective-permute-start = (bf16[2,128,768]{2,1,0:T(8,128)(2,1)S(1)}, bf16[2,128,768]{2,1,0:T(8,128)(2,1)S(1)}, u32[]{:S(2)}, u32[]{:S(2)}) collective-permute-start(bf16[2,128,768]{2,1,0:T(8,128)(2,1)S(1)} %pad_maximum_fusion.3), channel_id=1, source_target_pairs={{0,256},{256,0},{1,257},{257,1},{2,258},{258,2},{3,259},{259,3},{4... | collective-permute-start | bytes 1179656 | tf_op jit(solution)/shard_map/ppermute | solution.py:35
  36.4 0.5 convolution_bitcast_fusion.2
  37.0 0.3 convolution_bitcast_fusion.3
  37.3 2.4 %all_gather.13 = bf16[512,768]{1,0:T(8,128)(2,1)S(1)} all-gather(bf16[256,768]{1,0:T(8,128)(2,1)S(1)} %collective-permute-done.1), channel_id=1, replica_groups=mesh['xl'=2,'y'=8,'z'=8,'xh'=2,'c'=2] {'c'}, dimensions={0}, use_global_device_ids=true | all-gather | bytes 1179648 | tf_op jit(solution)/shard_map/all_gather | solution.py:31
  39.7 0.5 fusion.4
  40.3 0.3 fusion.3
  40.7 3.3 %collective-permute-start.2 = (bf16[2,128,768]{2,1,0:T(8,128)(2,1)S(1)}, bf16[2,128,768]{2,1,0:T(8,128)(2,1)S(1)}, u32[]{:S(2)}, u32[]{:S(2)}) collective-permute-start(bf16[2,128,768]{2,1,0:T(8,128)(2,1)S(1)} %pad_maximum_fusion.4), channel_id=1, source_target_pairs={{0,256},{256,0},{1,257},{257,1},{2,258},{258,2},{3,259},{259,3},{4... | collective-permute-start | bytes 1179656 | tf_op jit(solution)/shard_map/ppermute | solution.py:35
  44.0 0.5 convolution_bitcast_fusion
  44.6 0.3 convolution_bitcast_fusion.1
  44.9 2.9 %collective-permute-done = bf16[2,128,768]{2,1,0:T(8,128)(2,1)S(1)} collective-permute-done((bf16[2,128,768]{2,1,0:T(8,128)(2,1)S(1)}, bf16[2,128,768]{2,1,0:T(8,128)(2,1)S(1)}, u32[]{:S(2)}, u32[]{:S(2)}) %collective-permute-start) | collective-permute-done | bytes 393248 | tf_op jit(solution)/shard_map/ppermute | solution.py:35
  47.8 0.1 fusion.5
  47.8 7.5 %collective-permute-done.2 = bf16[2,128,768]{2,1,0:T(8,128)(2,1)S(1)} collective-permute-done((bf16[2,128,768]{2,1,0:T(8,128)(2,1)S(1)}, bf16[2,128,768]{2,1,0:T(8,128)(2,1)S(1)}, u32[]{:S(2)}, u32[]{:S(2)}) %collective-permute-start.2) | collective-permute-done | bytes 393248 | tf_op jit(solution)/shard_map/ppermute | solution.py:35
  55.4 0.1 fusion.6
  55.5 0.1 pad_maximum_fusion
  55.5 0.1 copy.15
  55.6 29.5 %all_to_all.45 = bf16[8,64,768]{2,1,0:T(8,128)(2,1)S(1)} all-to-all(bf16[8,64,768]{2,1,0:T(8,128)(2,1)S(1)} %bitcast.84), channel_id=1, replica_groups=mesh['xl'=2,'y'=8,'z'=8,'xh'=2,'c'=2] {'y'}, dimensions={0} | all-to-all | bytes 1572864 | tf_op jit(solution)/shard_map/all_to_all | solution.py:22
  85.1 0.1 convert_reduce_fusion
  85.2 0.7 multiply_convert_fusion
  85.9 1.0 broadcast_in_dim.10
  86.9 3.6 %all-to-all-start.2 = ((bf16[16,32,768]{2,1,0:T(8,128)(2,1)}), bf16[16,32,768]{2,1,0:T(8,128)(2,1)S(1)}, u32[]{:S(2)}, u32[]{:S(2)}) async-start(bf16[16,32,768]{2,1,0:T(8,128)(2,1)} %broadcast_in_dim.10), calls=%async_computation.2 | async-start | bytes 1572864 | tf_op jit(solution)/shard_map/all_to_all | solution.py:22
  90.5 1.0 pad_maximum_fusion.1
  91.5 1.0 pad_maximum_fusion.2
  92.4 17.4 %all-to-all-done.2 = bf16[16,32,768]{2,1,0:T(8,128)(2,1)S(1)} async-done(((bf16[16,32,768]{2,1,0:T(8,128)(2,1)}), bf16[16,32,768]{2,1,0:T(8,128)(2,1)S(1)}, u32[]{:S(2)}, u32[]{:S(2)}) %all-to-all-start.2) | async-done | bytes 786464 | tf_op jit(solution)/shard_map/all_to_all | solution.py:22
  109.8 0.8 broadcast_in_dim.11
  110.6 4.1 %all-to-all-start.3 = ((bf16[8,32,768]{2,1,0:T(8,128)(2,1)}), bf16[8,32,768]{2,1,0:T(8,128)(2,1)}, u32[]{:S(2)}, u32[]{:S(2)}) async-start(bf16[8,32,768]{2,1,0:T(8,128)(2,1)} %broadcast_in_dim.11), calls=%async_computation.3 | async-start | bytes 786432 | tf_op jit(solution)/shard_map/all_to_all | solution.py:22
  114.7 0.1 constant_dynamic-slice_fusion.2
  114.8 0.2 fusion.7
  115.0 0.5 fusion.42
  115.5 0.1 fusion.39
  115.6 2.4 %all_gather.14 = f32[256,768]{1,0:T(8,128)S(1)} all-gather(f32[128,768]{1,0:T(8,128)S(1)} %get-tuple-element.11), channel_id=1, replica_groups=mesh['xl'=2,'y'=8,'z'=8,'xh'=2,'c'=2] {'c'}, dimensions={0}, use_global_device_ids=true | all-gather | bytes 1179648 | tf_op jit(solution)/shard_map/all_gather | solution.py:31
  118.0 2.4 %all_gather.15 = f32[256,768]{1,0:T(8,128)S(1)} all-gather(f32[128,768]{1,0:T(8,128)S(1)} %get-tuple-element.12), channel_id=1, replica_groups=mesh['xl'=2,'y'=8,'z'=8,'xh'=2,'c'=2] {'c'}, dimensions={0}, use_global_device_ids=true | all-gather | bytes 1179648 | tf_op jit(solution)/shard_map/all_gather | solution.py:31
  120.4 1.3 fusion
  121.7 5.6 %all-to-all-done.3 = bf16[8,32,768]{2,1,0:T(8,128)(2,1)} async-done(((bf16[8,32,768]{2,1,0:T(8,128)(2,1)}), bf16[8,32,768]{2,1,0:T(8,128)(2,1)}, u32[]{:S(2)}, u32[]{:S(2)}) %all-to-all-start.3) | async-done | bytes 393248 | tf_op jit(solution)/shard_map/all_to_all | solution.py:22
  127.2 3.1 %collective-permute-start.3 = (bf16[256,768]{1,0:T(8,128)(2,1)}, bf16[256,768]{1,0:T(8,128)(2,1)S(1)}, u32[]{:S(2)}, u32[]{:S(2)}) collective-permute-start(bf16[256,768]{1,0:T(8,128)(2,1)} %bitcast.29), channel_id=1, source_target_pairs={{0,256},{256,0},{1,257},{257,1},{2,258},{258,2},{3,259},{259,3},{4... | collective-permute-start | bytes 1179656 | tf_op jit(solution)/shard_map/ppermute | solution.py:35
  130.3 7.3 %all-to-all-start.4 = ((bf16[16,16,768]{2,1,0:T(8,128)(2,1)}), bf16[16,16,768]{2,1,0:T(8,128)(2,1)S(1)}, u32[]{:S(2)}, u32[]{:S(2)}) async-start(bf16[16,16,768]{2,1,0:T(8,128)(2,1)} %bitcast.30), calls=%async_computation.4 | async-start | bytes 786432 | tf_op jit(solution)/shard_map/all_to_all | solution.py:22
  137.7 1.8 %convolution_convert_fusion = bf16[768,768]{1,0:T(8,128)(2,1)} fusion(bf16[512,768]{1,0:T(8,128)(2,1)S(1)} %bitcast.97, bf16[512,768]{1,0:T(8,128)(2,1)S(1)} %bitcast.86), kind=kOutput, calls=%fused_computation.2 | convolution fusion | flops 604569600 | bytes 2752512 | tf_op jit(solution)/shard_map/dot_general | solution.py:119
  139.5 1.5 %fusion.10 = f32[768,768]{1,0:T(8,128)S(1)} fusion(bf16[256,768]{1,0:T(8,128)(2,1)} %bitcast.29, bf16[2,256,768]{2,1,0:T(8,128)(2,1)S(1)} %bitcast.87, s32[]{:T(128)S(6)} %select_n.49), kind=kOutput, calls=%fused_computation.31 | convolution fusion | flops 301989888 | bytes 3145732 | tf_op jit(solution)/shard_map/dot_general | solution.py:119
  141.0 1.5 %add_convert_fusion = bf16[768,768]{1,0:T(8,128)(2,1)} fusion(f32[768,768]{1,0:T(8,128)S(1)} %fusion.10, bf16[256,768]{1,0:T(8,128)(2,1)S(1)} %collective-permute-done.3, bf16[2,256,768]{2,1,0:T(8,128)(2,1)S(1)} %bitcast.88, s32[]{:T(128)S(6)} %select_n.50), kind=kOutput, calls=%fused_computation | convolution fusion | flops 303169536 | bytes 4325380 | tf_op jit(solution)/shard_map/dot_general | solution.py:119
  142.6 6.7 %all-to-all-done.4 = bf16[16,16,768]{2,1,0:T(8,128)(2,1)S(1)} async-done(((bf16[16,16,768]{2,1,0:T(8,128)(2,1)}), bf16[16,16,768]{2,1,0:T(8,128)(2,1)S(1)}, u32[]{:S(2)}, u32[]{:S(2)}) %all-to-all-start.4) | async-done | bytes 393248 | tf_op jit(solution)/shard_map/all_to_all | solution.py:22
  149.2 0.7 reduce_sum.22
  (20 shorter events, 0.3 us)
Async XLA Ops:
  0.6 32.9 %copy-start = (bf16[768,768]{1,0:T(8,128)(2,1)S(1)}, bf16[768,768]{1,0:T(8,128)(2,1)}, u32[]{:S(2)}) copy-start(bf16[768,768]{1,0:T(8,128)(2,1)} %param.5) | copy-start | bytes 3538948
  2.3 23.2 %all-to-all-start = ((bf16[8,32,768]{2,1,0:T(8,128)(2,1)}), bf16[8,32,768]{2,1,0:T(8,128)(2,1)S(1)}, u32[]{:S(2)}, u32[]{:S(2)}) async-start(bf16[8,32,768]{2,1,0:T(8,128)(2,1)} %broadcast_in_dim.9), calls=%async_computation | async-start | bytes 786432 | tf_op jit(solution)/shard_map/all_to_all | solution.py:22
  25.5 7.5 %copy-start.1 = (bf16[768,768]{1,0:T(8,128)(2,1)S(1)}, bf16[768,768]{1,0:T(8,128)(2,1)}, u32[]{:S(2)}) copy-start(bf16[768,768]{1,0:T(8,128)(2,1)} %param.6) | copy-start | bytes 3538948
  25.5 11.8 %collective-permute-start.1 = (bf16[256,768]{1,0:T(8,128)(2,1)S(1)}, bf16[256,768]{1,0:T(8,128)(2,1)S(1)}, u32[]{:S(2)}, u32[]{:S(2)}) collective-permute-start(bf16[256,768]{1,0:T(8,128)(2,1)S(1)} %bitcast.90), channel_id=1, source_target_pairs={{0,2},{2,0},{1,3},{3,1},{4,6},{6,4},{5,7},{7,5},{8,10},{10,8},{9,1... | collective-permute-start | bytes 1179656 | tf_op jit(solution)/shard_map/ppermute | solution.py:35
  33.9 13.9 %collective-permute-start = (bf16[2,128,768]{2,1,0:T(8,128)(2,1)S(1)}, bf16[2,128,768]{2,1,0:T(8,128)(2,1)S(1)}, u32[]{:S(2)}, u32[]{:S(2)}) collective-permute-start(bf16[2,128,768]{2,1,0:T(8,128)(2,1)S(1)} %pad_maximum_fusion.3), channel_id=1, source_target_pairs={{0,256},{256,0},{1,257},{257,1},{2,258},{258,2},{3,259},{259,3},{4... | collective-permute-start | bytes 1179656 | tf_op jit(solution)/shard_map/ppermute | solution.py:35
  40.7 14.7 %collective-permute-start.2 = (bf16[2,128,768]{2,1,0:T(8,128)(2,1)S(1)}, bf16[2,128,768]{2,1,0:T(8,128)(2,1)S(1)}, u32[]{:S(2)}, u32[]{:S(2)}) collective-permute-start(bf16[2,128,768]{2,1,0:T(8,128)(2,1)S(1)} %pad_maximum_fusion.4), channel_id=1, source_target_pairs={{0,256},{256,0},{1,257},{257,1},{2,258},{258,2},{3,259},{259,3},{4... | collective-permute-start | bytes 1179656 | tf_op jit(solution)/shard_map/ppermute | solution.py:35
  86.9 22.9 %all-to-all-start.2 = ((bf16[16,32,768]{2,1,0:T(8,128)(2,1)}), bf16[16,32,768]{2,1,0:T(8,128)(2,1)S(1)}, u32[]{:S(2)}, u32[]{:S(2)}) async-start(bf16[16,32,768]{2,1,0:T(8,128)(2,1)} %broadcast_in_dim.10), calls=%async_computation.2 | async-start | bytes 1572864 | tf_op jit(solution)/shard_map/all_to_all | solution.py:22
  91.5 18.3 %copy-start.4 = (bf16[32,768]{1,0:T(8,128)(2,1)S(1)}, bf16[32,768]{1,0:T(8,128)(2,1)}, u32[]{:S(2)}) copy-start(bf16[32,768]{1,0:T(8,128)(2,1)} %get-tuple-element.19) | copy-start | bytes 147460
  110.6 16.7 %all-to-all-start.3 = ((bf16[8,32,768]{2,1,0:T(8,128)(2,1)}), bf16[8,32,768]{2,1,0:T(8,128)(2,1)}, u32[]{:S(2)}, u32[]{:S(2)}) async-start(bf16[8,32,768]{2,1,0:T(8,128)(2,1)} %broadcast_in_dim.11), calls=%async_computation.3 | async-start | bytes 786432 | tf_op jit(solution)/shard_map/all_to_all | solution.py:22
  120.4 17.3 %copy-start.3 = (bf16[16,2,16,768]{3,2,1,0:T(8,128)(2,1)S(1)}, bf16[16,2,16,768]{3,2,1,0:T(8,128)(2,1)}, u32[]{:S(2)}) copy-start(bf16[16,2,16,768]{3,2,1,0:T(8,128)(2,1)} %pad_maximum_fusion.1) | copy-start | bytes 2359300
  127.2 13.8 %collective-permute-start.3 = (bf16[256,768]{1,0:T(8,128)(2,1)}, bf16[256,768]{1,0:T(8,128)(2,1)S(1)}, u32[]{:S(2)}, u32[]{:S(2)}) collective-permute-start(bf16[256,768]{1,0:T(8,128)(2,1)} %bitcast.29), channel_id=1, source_target_pairs={{0,256},{256,0},{1,257},{257,1},{2,258},{258,2},{3,259},{259,3},{4... | collective-permute-start | bytes 1179656 | tf_op jit(solution)/shard_map/ppermute | solution.py:35
  130.3 18.9 %all-to-all-start.4 = ((bf16[16,16,768]{2,1,0:T(8,128)(2,1)}), bf16[16,16,768]{2,1,0:T(8,128)(2,1)S(1)}, u32[]{:S(2)}, u32[]{:S(2)}) async-start(bf16[16,16,768]{2,1,0:T(8,128)(2,1)} %bitcast.30), calls=%async_computation.4 | async-start | bytes 786432 | tf_op jit(solution)/shard_map/all_to_all | solution.py:22
  137.7 1.8 %copy-start.2 = (bf16[2,8,2,16,768]{4,3,2,1,0:T(8,128)(2,1)S(1)}, bf16[2,8,2,16,768]{4,3,2,1,0:T(8,128)(2,1)}, u32[]{:S(2)}) copy-start(bf16[2,8,2,16,768]{4,3,2,1,0:T(8,128)(2,1)} %pad_maximum_fusion.2) | copy-start | bytes 2359300

commit v6 on v5

--- a/solution.py
+++ b/solution.py
@@ -67,8 +67,9 @@
         sums = pre_and_back(whole_in, whole_grad, xl) + got.astype(f32)
         return sums.astype(bf16).reshape(2, 8, tokens, hidden)
 
-    both = jnp.stack([inputs, grad_out])
-    near = swap(jnp.broadcast_to(both[None], (8,) + both.shape).reshape(-1, width), "z")
+    which = lax.broadcasted_iota(jnp.int32, (8, 2, tokens, width), 1)
+    both = jnp.where(which == 0, inputs[None, None], grad_out[None, None])
+    near = swap(both.reshape(-1, width), "z")
     far = other(near, "xh")
     near_in, near_grad = over_cores(near)
     far_in, far_grad = over_cores(far)

time: 151 us -> 152 us (level)
  no operation moved by 1% of the time
where the time goes in v6:
time: 152 us; the launch traced here: 151 us
  waiting for transfers between devices  53.2 us (35%)
  starting transfers between devices  39 us (26%)
  blocking collectives  39 us (26%)
  matrix products  10.1 us (7%)
  other arithmetic  4.71 us (3%)
  local copies, waits for them, and re-layouts  3.91 us (3%)
    all_to_all x4, waiting for transfers between devices, swap(): return lax.all_to_all(blocks, axes, split_axis=0, concat_axis=0, tiled=True)  42.8 us
    all_to_all x1, blocking collectives, swap(): return lax.all_to_all(blocks, axes, split_axis=0, concat_axis=0, tiled=True)  29.5 us
    all_to_all x4, starting transfers between devices, swap(): return lax.all_to_all(blocks, axes, split_axis=0, concat_axis=0, tiled=True)  25 us
    ppermute x4, starting transfers between devices, other(): return lax.ppermute(block, axis, [(0, 1), (1, 0)])  14 us
    ppermute x4, waiting for transfers between devices, other(): return lax.ppermute(block, axis, [(0, 1), (1, 0)])  10.4 us
    all_gather x4, blocking collectives, gather(): return lax.all_gather(block, axis, axis=0, tiled=True)  9.48 us
    dot_general x3, matrix products, over_tokens(): lax.dot_general(left, right, (((0,), (0,)), ((), ())), preferred_element_...  4.88 us
  transfers between devices with their start and end apart: 8, of which 6 were waited for; matrix products, arithmetic and copies ran while one was open for 8% of the time, Pallas kernels for 0%

profile of v6, /device:TPU:64, one launch (start us, length us, event | category | flops | bytes accessed | tf_op | source)
XLA Modules:
  0.0 150.9 jit_solution(4734469779198437407)
XLA Ops:
  0.7 0.1 iota.11
  0.7 0.1 iota.12
  0.8 0.8 broadcast_in_dim.38
  1.7 0.7 broadcast_in_dim.41
  2.4 0.8 broadcast_select_fusion
  3.2 10.0 %all-to-all-start = ((bf16[8,32,768]{2,1,0:T(8,128)(2,1)}), bf16[8,32,768]{2,1,0:T(8,128)(2,1)S(1)}, u32[]{:S(2)}, u32[]{:S(2)}) async-start(bf16[8,32,768]{2,1,0:T(8,128)(2,1)} %broadcast_select_fusion), calls=%async_computation | async-start | bytes 786432 | tf_op jit(solution)/shard_map/all_to_all | solution.py:22
  13.2 13.2 %all-to-all-done = bf16[8,32,768]{2,1,0:T(8,128)(2,1)S(1)} async-done(((bf16[8,32,768]{2,1,0:T(8,128)(2,1)}), bf16[8,32,768]{2,1,0:T(8,128)(2,1)S(1)}, u32[]{:S(2)}, u32[]{:S(2)}) %all-to-all-start) | async-done | bytes 393248 | tf_op jit(solution)/shard_map/all_to_all | solution.py:22
  26.4 5.1 %collective-permute-start.1 = (bf16[256,768]{1,0:T(8,128)(2,1)S(1)}, bf16[256,768]{1,0:T(8,128)(2,1)S(1)}, u32[]{:S(2)}, u32[]{:S(2)}) collective-permute-start(bf16[256,768]{1,0:T(8,128)(2,1)S(1)} %bitcast.89), channel_id=1, source_target_pairs={{0,2},{2,0},{1,3},{3,1},{4,6},{6,4},{5,7},{7,5},{8,10},{10,8},{9,1... | collective-permute-start | bytes 1179656 | tf_op jit(solution)/shard_map/ppermute | solution.py:35
  31.5 2.4 %all_gather.12 = bf16[512,768]{1,0:T(8,128)(2,1)S(1)} all-gather(bf16[256,768]{1,0:T(8,128)(2,1)S(1)} %bitcast.90), channel_id=1, replica_groups=mesh['xl'=2,'y'=8,'z'=8,'xh'=2,'c'=2] {'c'}, dimensions={0}, use_global_device_ids=true | all-gather | bytes 1179648 | tf_op jit(solution)/shard_map/all_gather | solution.py:31
  33.9 0.5 fusion.2
  34.5 0.3 fusion.1
  34.9 2.5 %collective-permute-start = (bf16[2,128,768]{2,1,0:T(8,128)(2,1)S(1)}, bf16[2,128,768]{2,1,0:T(8,128)(2,1)S(1)}, u32[]{:S(2)}, u32[]{:S(2)}) collective-permute-start(bf16[2,128,768]{2,1,0:T(8,128)(2,1)S(1)} %pad_maximum_fusion.3), channel_id=1, source_target_pairs={{0,256},{256,0},{1,257},{257,1},{2,258},{258,2},{3,259},{259,3},{4... | collective-permute-start | bytes 1179656 | tf_op jit(solution)/shard_map/ppermute | solution.py:35
  37.4 0.5 convolution_bitcast_fusion.2
  37.9 0.3 convolution_bitcast_fusion.3
  38.3 2.4 %all_gather.13 = bf16[512,768]{1,0:T(8,128)(2,1)S(1)} all-gather(bf16[256,768]{1,0:T(8,128)(2,1)S(1)} %collective-permute-done.1), channel_id=1, replica_groups=mesh['xl'=2,'y'=8,'z'=8,'xh'=2,'c'=2] {'c'}, dimensions={0}, use_global_device_ids=true | all-gather | bytes 1179648 | tf_op jit(solution)/shard_map/all_gather | solution.py:31
  40.7 0.5 fusion.4
  41.2 0.3 fusion.3
  41.6 3.3 %collective-permute-start.2 = (bf16[2,128,768]{2,1,0:T(8,128)(2,1)S(1)}, bf16[2,128,768]{2,1,0:T(8,128)(2,1)S(1)}, u32[]{:S(2)}, u32[]{:S(2)}) collective-permute-start(bf16[2,128,768]{2,1,0:T(8,128)(2,1)S(1)} %pad_maximum_fusion.4), channel_id=1, source_target_pairs={{0,256},{256,0},{1,257},{257,1},{2,258},{258,2},{3,259},{259,3},{4... | collective-permute-start | bytes 1179656 | tf_op jit(solution)/shard_map/ppermute | solution.py:35
  45.0 0.5 convolution_bitcast_fusion
  45.5 0.3 convolution_bitcast_fusion.1
  45.8 2.9 %collective-permute-done = bf16[2,128,768]{2,1,0:T(8,128)(2,1)S(1)} collective-permute-done((bf16[2,128,768]{2,1,0:T(8,128)(2,1)S(1)}, bf16[2,128,768]{2,1,0:T(8,128)(2,1)S(1)}, u32[]{:S(2)}, u32[]{:S(2)}) %collective-permute-start) | collective-permute-done | bytes 393248 | tf_op jit(solution)/shard_map/ppermute | solution.py:35
  48.7 0.1 fusion.5
  48.8 7.5 %collective-permute-done.2 = bf16[2,128,768]{2,1,0:T(8,128)(2,1)S(1)} collective-permute-done((bf16[2,128,768]{2,1,0:T(8,128)(2,1)S(1)}, bf16[2,128,768]{2,1,0:T(8,128)(2,1)S(1)}, u32[]{:S(2)}, u32[]{:S(2)}) %collective-permute-start.2) | collective-permute-done | bytes 393248 | tf_op jit(solution)/shard_map/ppermute | solution.py:35
  56.4 0.1 pad_maximum_fusion
  56.5 0.1 copy.15
  56.6 29.5 %all_to_all.45 = bf16[8,64,768]{2,1,0:T(8,128)(2,1)S(1)} all-to-all(bf16[8,64,768]{2,1,0:T(8,128)(2,1)S(1)} %bitcast.83), channel_id=1, replica_groups=mesh['xl'=2,'y'=8,'z'=8,'xh'=2,'c'=2] {'y'}, dimensions={0} | all-to-all | bytes 1572864 | tf_op jit(solution)/shard_map/all_to_all | solution.py:22
  86.1 0.1 convert_reduce_fusion
  86.2 0.7 multiply_convert_fusion
  86.9 1.0 broadcast_in_dim.44
  87.8 3.6 %all-to-all-start.2 = ((bf16[16,32,768]{2,1,0:T(8,128)(2,1)}), bf16[16,32,768]{2,1,0:T(8,128)(2,1)S(1)}, u32[]{:S(2)}, u32[]{:S(2)}) async-start(bf16[16,32,768]{2,1,0:T(8,128)(2,1)} %broadcast_in_dim.44), calls=%async_computation.2 | async-start | bytes 1572864 | tf_op jit(solution)/shard_map/all_to_all | solution.py:22
  91.5 1.0 pad_maximum_fusion.1
  92.4 1.0 pad_maximum_fusion.2
  93.4 17.4 %all-to-all-done.2 = bf16[16,32,768]{2,1,0:T(8,128)(2,1)S(1)} async-done(((bf16[16,32,768]{2,1,0:T(8,128)(2,1)}), bf16[16,32,768]{2,1,0:T(8,128)(2,1)S(1)}, u32[]{:S(2)}, u32[]{:S(2)}) %all-to-all-start.2) | async-done | bytes 786464 | tf_op jit(solution)/shard_map/all_to_all | solution.py:22
  110.8 0.8 broadcast_in_dim.45
  111.5 4.1 %all-to-all-start.3 = ((bf16[8,32,768]{2,1,0:T(8,128)(2,1)}), bf16[8,32,768]{2,1,0:T(8,128)(2,1)}, u32[]{:S(2)}, u32[]{:S(2)}) async-start(bf16[8,32,768]{2,1,0:T(8,128)(2,1)} %broadcast_in_dim.45), calls=%async_computation.3 | async-start | bytes 786432 | tf_op jit(solution)/shard_map/all_to_all | solution.py:22
  115.7 0.2 fusion.7
  116.0 0.5 fusion.42
  116.5 2.4 %all_gather.14 = f32[256,768]{1,0:T(8,128)S(1)} all-gather(f32[128,768]{1,0:T(8,128)S(1)} %get-tuple-element.11), channel_id=1, replica_groups=mesh['xl'=2,'y'=8,'z'=8,'xh'=2,'c'=2] {'c'}, dimensions={0}, use_global_device_ids=true | all-gather | bytes 1179648 | tf_op jit(solution)/shard_map/all_gather | solution.py:31
  118.9 2.4 %all_gather.15 = f32[256,768]{1,0:T(8,128)S(1)} all-gather(f32[128,768]{1,0:T(8,128)S(1)} %get-tuple-element.12), channel_id=1, replica_groups=mesh['xl'=2,'y'=8,'z'=8,'xh'=2,'c'=2] {'c'}, dimensions={0}, use_global_device_ids=true | all-gather | bytes 1179648 | tf_op jit(solution)/shard_map/all_gather | solution.py:31
  121.3 1.3 fusion
  122.6 5.6 %all-to-all-done.3 = bf16[8,32,768]{2,1,0:T(8,128)(2,1)} async-done(((bf16[8,32,768]{2,1,0:T(8,128)(2,1)}), bf16[8,32,768]{2,1,0:T(8,128)(2,1)}, u32[]{:S(2)}, u32[]{:S(2)}) %all-to-all-start.3) | async-done | bytes 393248 | tf_op jit(solution)/shard_map/all_to_all | solution.py:22
  128.2 3.1 %collective-permute-start.3 = (bf16[256,768]{1,0:T(8,128)(2,1)}, bf16[256,768]{1,0:T(8,128)(2,1)S(1)}, u32[]{:S(2)}, u32[]{:S(2)}) collective-permute-start(bf16[256,768]{1,0:T(8,128)(2,1)} %bitcast.28), channel_id=1, source_target_pairs={{0,256},{256,0},{1,257},{257,1},{2,258},{258,2},{3,259},{259,3},{4... | collective-permute-start | bytes 1179656 | tf_op jit(solution)/shard_map/ppermute | solution.py:35
  131.3 7.4 %all-to-all-start.4 = ((bf16[16,16,768]{2,1,0:T(8,128)(2,1)}), bf16[16,16,768]{2,1,0:T(8,128)(2,1)S(1)}, u32[]{:S(2)}, u32[]{:S(2)}) async-start(bf16[16,16,768]{2,1,0:T(8,128)(2,1)} %bitcast.29), calls=%async_computation.4 | async-start | bytes 786432 | tf_op jit(solution)/shard_map/all_to_all | solution.py:22
  138.7 1.8 %convolution_convert_fusion = bf16[768,768]{1,0:T(8,128)(2,1)} fusion(bf16[512,768]{1,0:T(8,128)(2,1)S(1)} %bitcast.96, bf16[512,768]{1,0:T(8,128)(2,1)S(1)} %bitcast.85), kind=kOutput, calls=%fused_computation.2 | convolution fusion | flops 604569600 | bytes 2752512 | tf_op jit(solution)/shard_map/dot_general | solution.py:120
  140.5 1.5 %fusion.10 = f32[768,768]{1,0:T(8,128)S(1)} fusion(bf16[256,768]{1,0:T(8,128)(2,1)} %bitcast.28, bf16[2,256,768]{2,1,0:T(8,128)(2,1)S(1)} %bitcast.86, s32[]{:T(128)S(6)} %select_n.56), kind=kOutput, calls=%fused_computation.31 | convolution fusion | flops 301989888 | bytes 3145732 | tf_op jit(solution)/shard_map/dot_general | solution.py:120
  142.0 1.5 %add_convert_fusion = bf16[768,768]{1,0:T(8,128)(2,1)} fusion(f32[768,768]{1,0:T(8,128)S(1)} %fusion.10, bf16[256,768]{1,0:T(8,128)(2,1)S(1)} %collective-permute-done.3, bf16[2,256,768]{2,1,0:T(8,128)(2,1)S(1)} %bitcast.87, s32[]{:T(128)S(6)} %select_n.57), kind=kOutput, calls=%fused_computation | convolution fusion | flops 303169536 | bytes 4325380 | tf_op jit(solution)/shard_map/dot_general | solution.py:120
  143.6 6.7 %all-to-all-done.4 = bf16[16,16,768]{2,1,0:T(8,128)(2,1)S(1)} async-done(((bf16[16,16,768]{2,1,0:T(8,128)(2,1)}), bf16[16,16,768]{2,1,0:T(8,128)(2,1)S(1)}, u32[]{:S(2)}, u32[]{:S(2)}) %all-to-all-start.4) | async-done | bytes 393248 | tf_op jit(solution)/shard_map/all_to_all | solution.py:22
  150.2 0.7 reduce_sum.22
  (24 shorter events, 0.5 us)
Async XLA Ops:
  0.6 33.8 %copy-start = (bf16[768,768]{1,0:T(8,128)(2,1)S(1)}, bf16[768,768]{1,0:T(8,128)(2,1)}, u32[]{:S(2)}) copy-start(bf16[768,768]{1,0:T(8,128)(2,1)} %param.5) | copy-start | bytes 3538948
  3.2 23.2 %all-to-all-start = ((bf16[8,32,768]{2,1,0:T(8,128)(2,1)}), bf16[8,32,768]{2,1,0:T(8,128)(2,1)S(1)}, u32[]{:S(2)}, u32[]{:S(2)}) async-start(bf16[8,32,768]{2,1,0:T(8,128)(2,1)} %broadcast_select_fusion), calls=%async_computation | async-start | bytes 786432 | tf_op jit(solution)/shard_map/all_to_all | solution.py:22
  26.4 7.5 %copy-start.1 = (bf16[768,768]{1,0:T(8,128)(2,1)S(1)}, bf16[768,768]{1,0:T(8,128)(2,1)}, u32[]{:S(2)}) copy-start(bf16[768,768]{1,0:T(8,128)(2,1)} %param.6) | copy-start | bytes 3538948
  26.4 11.8 %collective-permute-start.1 = (bf16[256,768]{1,0:T(8,128)(2,1)S(1)}, bf16[256,768]{1,0:T(8,128)(2,1)S(1)}, u32[]{:S(2)}, u32[]{:S(2)}) collective-permute-start(bf16[256,768]{1,0:T(8,128)(2,1)S(1)} %bitcast.89), channel_id=1, source_target_pairs={{0,2},{2,0},{1,3},{3,1},{4,6},{6,4},{5,7},{7,5},{8,10},{10,8},{9,1... | collective-permute-start | bytes 1179656 | tf_op jit(solution)/shard_map/ppermute | solution.py:35
  34.9 13.9 %collective-permute-start = (bf16[2,128,768]{2,1,0:T(8,128)(2,1)S(1)}, bf16[2,128,768]{2,1,0:T(8,128)(2,1)S(1)}, u32[]{:S(2)}, u32[]{:S(2)}) collective-permute-start(bf16[2,128,768]{2,1,0:T(8,128)(2,1)S(1)} %pad_maximum_fusion.3), channel_id=1, source_target_pairs={{0,256},{256,0},{1,257},{257,1},{2,258},{258,2},{3,259},{259,3},{4... | collective-permute-start | bytes 1179656 | tf_op jit(solution)/shard_map/ppermute | solution.py:35
  41.6 14.7 %collective-permute-start.2 = (bf16[2,128,768]{2,1,0:T(8,128)(2,1)S(1)}, bf16[2,128,768]{2,1,0:T(8,128)(2,1)S(1)}, u32[]{:S(2)}, u32[]{:S(2)}) collective-permute-start(bf16[2,128,768]{2,1,0:T(8,128)(2,1)S(1)} %pad_maximum_fusion.4), channel_id=1, source_target_pairs={{0,256},{256,0},{1,257},{257,1},{2,258},{258,2},{3,259},{259,3},{4... | collective-permute-start | bytes 1179656 | tf_op jit(solution)/shard_map/ppermute | solution.py:35
  87.8 22.9 %all-to-all-start.2 = ((bf16[16,32,768]{2,1,0:T(8,128)(2,1)}), bf16[16,32,768]{2,1,0:T(8,128)(2,1)S(1)}, u32[]{:S(2)}, u32[]{:S(2)}) async-start(bf16[16,32,768]{2,1,0:T(8,128)(2,1)} %broadcast_in_dim.44), calls=%async_computation.2 | async-start | bytes 1572864 | tf_op jit(solution)/shard_map/all_to_all | solution.py:22
  92.4 18.3 %copy-start.4 = (bf16[32,768]{1,0:T(8,128)(2,1)S(1)}, bf16[32,768]{1,0:T(8,128)(2,1)}, u32[]{:S(2)}) copy-start(bf16[32,768]{1,0:T(8,128)(2,1)} %get-tuple-element.19) | copy-start | bytes 147460
  111.5 16.7 %all-to-all-start.3 = ((bf16[8,32,768]{2,1,0:T(8,128)(2,1)}), bf16[8,32,768]{2,1,0:T(8,128)(2,1)}, u32[]{:S(2)}, u32[]{:S(2)}) async-start(bf16[8,32,768]{2,1,0:T(8,128)(2,1)} %broadcast_in_dim.45), calls=%async_computation.3 | async-start | bytes 786432 | tf_op jit(solution)/shard_map/all_to_all | solution.py:22
  121.3 17.3 %copy-start.3 = (bf16[16,2,16,768]{3,2,1,0:T(8,128)(2,1)S(1)}, bf16[16,2,16,768]{3,2,1,0:T(8,128)(2,1)}, u32[]{:S(2)}) copy-start(bf16[16,2,16,768]{3,2,1,0:T(8,128)(2,1)} %pad_maximum_fusion.1) | copy-start | bytes 2359300
  128.2 13.8 %collective-permute-start.3 = (bf16[256,768]{1,0:T(8,128)(2,1)}, bf16[256,768]{1,0:T(8,128)(2,1)S(1)}, u32[]{:S(2)}, u32[]{:S(2)}) collective-permute-start(bf16[256,768]{1,0:T(8,128)(2,1)} %bitcast.28), channel_id=1, source_target_pairs={{0,256},{256,0},{1,257},{257,1},{2,258},{258,2},{3,259},{259,3},{4... | collective-permute-start | bytes 1179656 | tf_op jit(solution)/shard_map/ppermute | solution.py:35
  131.3 18.9 %all-to-all-start.4 = ((bf16[16,16,768]{2,1,0:T(8,128)(2,1)}), bf16[16,16,768]{2,1,0:T(8,128)(2,1)S(1)}, u32[]{:S(2)}, u32[]{:S(2)}) async-start(bf16[16,16,768]{2,1,0:T(8,128)(2,1)} %bitcast.29), calls=%async_computation.4 | async-start | bytes 786432 | tf_op jit(solution)/shard_map/all_to_all | solution.py:22
  138.6 1.8 %copy-start.2 = (bf16[2,8,2,16,768]{4,3,2,1,0:T(8,128)(2,1)S(1)}, bf16[2,8,2,16,768]{4,3,2,1,0:T(8,128)(2,1)}, u32[]{:S(2)}) copy-start(bf16[2,8,2,16,768]{4,3,2,1,0:T(8,128)(2,1)} %pad_maximum_fusion.2) | copy-start | bytes 2359300

commit v7 on v5

--- a/solution.py
+++ b/solution.py
@@ -101,8 +101,7 @@
         return half(both, 1 - core)
 
     given, kept = in_of(1 - core), in_of(core)
-    size = given.shape[0] // 2
-    got = jnp.concatenate([got_from(given[:size]), got_from(given[size:])])
+    got = got_from(given.astype(bf16)).astype(f32)
     kept = (kept + got).astype(bf16)
     kept, act_mine = lax.optimization_barrier((kept, act_mine))
     pieces = swap(kept, ("xh", "z")).reshape(16, tokens, width)

time: 151 us -> 151 us (level)
  waiting for transfers between devices: 53.2 us -> 55.8 us
  blocking collectives: 39 us -> 36.6 us
    all_to_all x4, waiting for transfers between devices: 42.8 us -> 45.3 us  [swap(): return lax.all_to_all(blocks, axes, split_axis=0, concat_axis=0, tiled=True)]
    all_gather x4 -> x3, blocking collectives: 9.48 us -> 7.11 us  [gather(): return lax.all_gather(block, axis, axis=0, tiled=True)]
where the time goes in v7:
time: 151 us; the launch traced here: 150 us
  waiting for transfers between devices  55.8 us (37%)
  starting transfers between devices  39 us (26%)
  blocking collectives  36.6 us (24%)
  matrix products  10.1 us (7%)
  other arithmetic  4.71 us (3%)
  local copies, waits for them, and re-layouts  2.84 us (2%)
    all_to_all x4, waiting for transfers between devices, swap(): return lax.all_to_all(blocks, axes, split_axis=0, concat_axis=0, tiled=True)  45.3 us
    all_to_all x1, blocking collectives, swap(): return lax.all_to_all(blocks, axes, split_axis=0, concat_axis=0, tiled=True)  29.5 us
    all_to_all x4, starting transfers between devices, swap(): return lax.all_to_all(blocks, axes, split_axis=0, concat_axis=0, tiled=True)  25 us
    ppermute x4, starting transfers between devices, other(): return lax.ppermute(block, axis, [(0, 1), (1, 0)])  14 us
    ppermute x4, waiting for transfers between devices, other(): return lax.ppermute(block, axis, [(0, 1), (1, 0)])  10.4 us
    all_gather x3, blocking collectives, gather(): return lax.all_gather(block, axis, axis=0, tiled=True)  7.11 us
    dot_general x3, matrix products, over_tokens(): lax.dot_general(left, right, (((0,), (0,)), ((), ())), preferred_element_...  4.88 us
  transfers between devices with their start and end apart: 8, of which 6 were waited for; matrix products, arithmetic and copies ran while one was open for 8% of the time, Pallas kernels for 0%

profile of v7, /device:TPU:64, one launch (start us, length us, event | category | flops | bytes accessed | tf_op | source)
XLA Modules:
  0.0 149.9 jit_solution(8828551253444976562)
XLA Ops:
  0.6 0.9 pad_maximum_fusion.5
  1.5 0.8 broadcast_in_dim.9
  2.3 10.0 %all-to-all-start = ((bf16[8,32,768]{2,1,0:T(8,128)(2,1)}), bf16[8,32,768]{2,1,0:T(8,128)(2,1)S(1)}, u32[]{:S(2)}, u32[]{:S(2)}) async-start(bf16[8,32,768]{2,1,0:T(8,128)(2,1)} %broadcast_in_dim.9), calls=%async_computation | async-start | bytes 786432 | tf_op jit(solution)/shard_map/all_to_all | solution.py:22
  12.2 13.2 %all-to-all-done = bf16[8,32,768]{2,1,0:T(8,128)(2,1)S(1)} async-done(((bf16[8,32,768]{2,1,0:T(8,128)(2,1)}), bf16[8,32,768]{2,1,0:T(8,128)(2,1)S(1)}, u32[]{:S(2)}, u32[]{:S(2)}) %all-to-all-start) | async-done | bytes 393248 | tf_op jit(solution)/shard_map/all_to_all | solution.py:22
  25.5 5.1 %collective-permute-start.1 = (bf16[256,768]{1,0:T(8,128)(2,1)S(1)}, bf16[256,768]{1,0:T(8,128)(2,1)S(1)}, u32[]{:S(2)}, u32[]{:S(2)}) collective-permute-start(bf16[256,768]{1,0:T(8,128)(2,1)S(1)} %bitcast.90), channel_id=1, source_target_pairs={{0,2},{2,0},{1,3},{3,1},{4,6},{6,4},{5,7},{7,5},{8,10},{10,8},{9,1... | collective-permute-start | bytes 1179656 | tf_op jit(solution)/shard_map/ppermute | solution.py:35
  30.5 2.4 %all_gather.9 = bf16[512,768]{1,0:T(8,128)(2,1)S(1)} all-gather(bf16[256,768]{1,0:T(8,128)(2,1)S(1)} %bitcast.91), channel_id=1, replica_groups=mesh['xl'=2,'y'=8,'z'=8,'xh'=2,'c'=2] {'c'}, dimensions={0}, use_global_device_ids=true | all-gather | bytes 1179648 | tf_op jit(solution)/shard_map/all_gather | solution.py:31
  32.9 0.1 fusion.39
  33.0 0.5 fusion.2
  33.5 0.3 fusion.1
  33.9 2.5 %collective-permute-start = (bf16[2,128,768]{2,1,0:T(8,128)(2,1)S(1)}, bf16[2,128,768]{2,1,0:T(8,128)(2,1)S(1)}, u32[]{:S(2)}, u32[]{:S(2)}) collective-permute-start(bf16[2,128,768]{2,1,0:T(8,128)(2,1)S(1)} %pad_maximum_fusion.3), channel_id=1, source_target_pairs={{0,256},{256,0},{1,257},{257,1},{2,258},{258,2},{3,259},{259,3},{4... | collective-permute-start | bytes 1179656 | tf_op jit(solution)/shard_map/ppermute | solution.py:35
  36.4 0.5 convolution_bitcast_fusion.2
  37.0 0.3 convolution_bitcast_fusion.3
  37.3 2.4 %all_gather.10 = bf16[512,768]{1,0:T(8,128)(2,1)S(1)} all-gather(bf16[256,768]{1,0:T(8,128)(2,1)S(1)} %collective-permute-done.1), channel_id=1, replica_groups=mesh['xl'=2,'y'=8,'z'=8,'xh'=2,'c'=2] {'c'}, dimensions={0}, use_global_device_ids=true | all-gather | bytes 1179648 | tf_op jit(solution)/shard_map/all_gather | solution.py:31
  39.7 0.1 fusion.40
  39.7 0.5 fusion.4
  40.3 0.3 fusion.3
  40.7 3.3 %collective-permute-start.2 = (bf16[2,128,768]{2,1,0:T(8,128)(2,1)S(1)}, bf16[2,128,768]{2,1,0:T(8,128)(2,1)S(1)}, u32[]{:S(2)}, u32[]{:S(2)}) collective-permute-start(bf16[2,128,768]{2,1,0:T(8,128)(2,1)S(1)} %pad_maximum_fusion.4), channel_id=1, source_target_pairs={{0,256},{256,0},{1,257},{257,1},{2,258},{258,2},{3,259},{259,3},{4... | collective-permute-start | bytes 1179656 | tf_op jit(solution)/shard_map/ppermute | solution.py:35
  44.0 0.5 convolution_bitcast_fusion
  44.6 0.3 convolution_bitcast_fusion.1
  44.9 2.9 %collective-permute-done = bf16[2,128,768]{2,1,0:T(8,128)(2,1)S(1)} collective-permute-done((bf16[2,128,768]{2,1,0:T(8,128)(2,1)S(1)}, bf16[2,128,768]{2,1,0:T(8,128)(2,1)S(1)}, u32[]{:S(2)}, u32[]{:S(2)}) %collective-permute-start) | collective-permute-done | bytes 393248 | tf_op jit(solution)/shard_map/ppermute | solution.py:35
  47.8 0.1 fusion.5
  47.8 7.5 %collective-permute-done.2 = bf16[2,128,768]{2,1,0:T(8,128)(2,1)S(1)} collective-permute-done((bf16[2,128,768]{2,1,0:T(8,128)(2,1)S(1)}, bf16[2,128,768]{2,1,0:T(8,128)(2,1)S(1)}, u32[]{:S(2)}, u32[]{:S(2)}) %collective-permute-start.2) | collective-permute-done | bytes 393248 | tf_op jit(solution)/shard_map/ppermute | solution.py:35
  55.4 0.1 fusion.6
  55.5 0.1 pad_maximum_fusion
  55.5 0.1 copy.15
  55.6 29.5 %all_to_all.45 = bf16[8,64,768]{2,1,0:T(8,128)(2,1)S(1)} all-to-all(bf16[8,64,768]{2,1,0:T(8,128)(2,1)S(1)} %bitcast.84), channel_id=1, replica_groups=mesh['xl'=2,'y'=8,'z'=8,'xh'=2,'c'=2] {'y'}, dimensions={0} | all-to-all | bytes 1572864 | tf_op jit(solution)/shard_map/all_to_all | solution.py:22
  85.1 0.1 convert_reduce_fusion
  85.2 0.7 multiply_convert_fusion
  85.9 1.0 broadcast_in_dim.10
  86.9 3.6 %all-to-all-start.2 = ((bf16[16,32,768]{2,1,0:T(8,128)(2,1)}), bf16[16,32,768]{2,1,0:T(8,128)(2,1)S(1)}, u32[]{:S(2)}, u32[]{:S(2)}) async-start(bf16[16,32,768]{2,1,0:T(8,128)(2,1)} %broadcast_in_dim.10), calls=%async_computation.2 | async-start | bytes 1572864 | tf_op jit(solution)/shard_map/all_to_all | solution.py:22
  90.5 1.0 pad_maximum_fusion.1
  91.4 1.0 pad_maximum_fusion.2
  92.4 17.3 %all-to-all-done.2 = bf16[16,32,768]{2,1,0:T(8,128)(2,1)S(1)} async-done(((bf16[16,32,768]{2,1,0:T(8,128)(2,1)}), bf16[16,32,768]{2,1,0:T(8,128)(2,1)S(1)}, u32[]{:S(2)}, u32[]{:S(2)}) %all-to-all-start.2) | async-done | bytes 786464 | tf_op jit(solution)/shard_map/all_to_all | solution.py:22
  109.8 0.8 broadcast_in_dim.11
  110.6 4.1 %all-to-all-start.3 = ((bf16[8,32,768]{2,1,0:T(8,128)(2,1)}), bf16[8,32,768]{2,1,0:T(8,128)(2,1)}, u32[]{:S(2)}, u32[]{:S(2)}) async-start(bf16[8,32,768]{2,1,0:T(8,128)(2,1)} %broadcast_in_dim.11), calls=%async_computation.3 | async-start | bytes 786432 | tf_op jit(solution)/shard_map/all_to_all | solution.py:22
  114.7 0.1 constant_dynamic-slice_fusion
  114.7 0.2 fusion.7
  115.0 0.5 convolution_convert_fusion.1
  115.5 2.4 %all_gather.11 = bf16[512,768]{1,0:T(8,128)(2,1)S(1)} all-gather(bf16[256,768]{1,0:T(8,128)(2,1)S(1)} %convolution_convert_fusion.1), channel_id=1, replica_groups=mesh['xl'=2,'y'=8,'z'=8,'xh'=2,'c'=2] {'c'}, dimensions={0}, use_global_device_ids=true | all-gather | bytes 1179648 | tf_op jit(solution)/shard_map/all_gather | solution.py:31
  117.9 1.3 fusion
  119.1 8.1 %all-to-all-done.3 = bf16[8,32,768]{2,1,0:T(8,128)(2,1)} async-done(((bf16[8,32,768]{2,1,0:T(8,128)(2,1)}), bf16[8,32,768]{2,1,0:T(8,128)(2,1)}, u32[]{:S(2)}, u32[]{:S(2)}) %all-to-all-start.3) | async-done | bytes 393248 | tf_op jit(solution)/shard_map/all_to_all | solution.py:22
  127.2 3.1 %collective-permute-start.3 = (bf16[256,768]{1,0:T(8,128)(2,1)}, bf16[256,768]{1,0:T(8,128)(2,1)S(1)}, u32[]{:S(2)}, u32[]{:S(2)}) collective-permute-start(bf16[256,768]{1,0:T(8,128)(2,1)} %bitcast.29), channel_id=1, source_target_pairs={{0,256},{256,0},{1,257},{257,1},{2,258},{258,2},{3,259},{259,3},{4... | collective-permute-start | bytes 1179656 | tf_op jit(solution)/shard_map/ppermute | solution.py:35
  130.3 7.3 %all-to-all-start.4 = ((bf16[16,16,768]{2,1,0:T(8,128)(2,1)}), bf16[16,16,768]{2,1,0:T(8,128)(2,1)S(1)}, u32[]{:S(2)}, u32[]{:S(2)}) async-start(bf16[16,16,768]{2,1,0:T(8,128)(2,1)} %bitcast.30), calls=%async_computation.4 | async-start | bytes 786432 | tf_op jit(solution)/shard_map/all_to_all | solution.py:22
  137.7 1.8 %convolution_convert_fusion = bf16[768,768]{1,0:T(8,128)(2,1)} fusion(bf16[512,768]{1,0:T(8,128)(2,1)S(1)} %bitcast.97, bf16[512,768]{1,0:T(8,128)(2,1)S(1)} %bitcast.86), kind=kOutput, calls=%fused_computation.2 | convolution fusion | flops 604569600 | bytes 2752512 | tf_op jit(solution)/shard_map/dot_general | solution.py:118
  139.5 1.5 %fusion.10 = f32[768,768]{1,0:T(8,128)S(1)} fusion(bf16[256,768]{1,0:T(8,128)(2,1)} %bitcast.29, bf16[2,256,768]{2,1,0:T(8,128)(2,1)S(1)} %bitcast.87, s32[]{:T(128)S(6)} %select_n.45), kind=kOutput, calls=%fused_computation.32 | convolution fusion | flops 301989888 | bytes 3145732 | tf_op jit(solution)/shard_map/dot_general | solution.py:118
  141.0 1.5 %add_convert_fusion = bf16[768,768]{1,0:T(8,128)(2,1)} fusion(f32[768,768]{1,0:T(8,128)S(1)} %fusion.10, bf16[256,768]{1,0:T(8,128)(2,1)S(1)} %collective-permute-done.3, bf16[2,256,768]{2,1,0:T(8,128)(2,1)S(1)} %bitcast.88, s32[]{:T(128)S(6)} %select_n.46), kind=kOutput, calls=%fused_computation | convolution fusion | flops 303169536 | bytes 4325380 | tf_op jit(solution)/shard_map/dot_general | solution.py:118
  142.6 6.7 %all-to-all-done.4 = bf16[16,16,768]{2,1,0:T(8,128)(2,1)S(1)} async-done(((bf16[16,16,768]{2,1,0:T(8,128)(2,1)}), bf16[16,16,768]{2,1,0:T(8,128)(2,1)S(1)}, u32[]{:S(2)}, u32[]{:S(2)}) %all-to-all-start.4) | async-done | bytes 393248 | tf_op jit(solution)/shard_map/all_to_all | solution.py:22
  149.2 0.7 reduce_sum.22
  (16 shorter events, 0.2 us)
Async XLA Ops:
  0.6 32.9 %copy-start = (bf16[768,768]{1,0:T(8,128)(2,1)S(1)}, bf16[768,768]{1,0:T(8,128)(2,1)}, u32[]{:S(2)}) copy-start(bf16[768,768]{1,0:T(8,128)(2,1)} %param.5) | copy-start | bytes 3538948
  2.3 23.2 %all-to-all-start = ((bf16[8,32,768]{2,1,0:T(8,128)(2,1)}), bf16[8,32,768]{2,1,0:T(8,128)(2,1)S(1)}, u32[]{:S(2)}, u32[]{:S(2)}) async-start(bf16[8,32,768]{2,1,0:T(8,128)(2,1)} %broadcast_in_dim.9), calls=%async_computation | async-start | bytes 786432 | tf_op jit(solution)/shard_map/all_to_all | solution.py:22
  25.5 7.5 %copy-start.1 = (bf16[768,768]{1,0:T(8,128)(2,1)S(1)}, bf16[768,768]{1,0:T(8,128)(2,1)}, u32[]{:S(2)}) copy-start(bf16[768,768]{1,0:T(8,128)(2,1)} %param.6) | copy-start | bytes 3538948
  25.5 11.8 %collective-permute-start.1 = (bf16[256,768]{1,0:T(8,128)(2,1)S(1)}, bf16[256,768]{1,0:T(8,128)(2,1)S(1)}, u32[]{:S(2)}, u32[]{:S(2)}) collective-permute-start(bf16[256,768]{1,0:T(8,128)(2,1)S(1)} %bitcast.90), channel_id=1, source_target_pairs={{0,2},{2,0},{1,3},{3,1},{4,6},{6,4},{5,7},{7,5},{8,10},{10,8},{9,1... | collective-permute-start | bytes 1179656 | tf_op jit(solution)/shard_map/ppermute | solution.py:35
  33.9 13.9 %collective-permute-start = (bf16[2,128,768]{2,1,0:T(8,128)(2,1)S(1)}, bf16[2,128,768]{2,1,0:T(8,128)(2,1)S(1)}, u32[]{:S(2)}, u32[]{:S(2)}) collective-permute-start(bf16[2,128,768]{2,1,0:T(8,128)(2,1)S(1)} %pad_maximum_fusion.3), channel_id=1, source_target_pairs={{0,256},{256,0},{1,257},{257,1},{2,258},{258,2},{3,259},{259,3},{4... | collective-permute-start | bytes 1179656 | tf_op jit(solution)/shard_map/ppermute | solution.py:35
  40.7 14.7 %collective-permute-start.2 = (bf16[2,128,768]{2,1,0:T(8,128)(2,1)S(1)}, bf16[2,128,768]{2,1,0:T(8,128)(2,1)S(1)}, u32[]{:S(2)}, u32[]{:S(2)}) collective-permute-start(bf16[2,128,768]{2,1,0:T(8,128)(2,1)S(1)} %pad_maximum_fusion.4), channel_id=1, source_target_pairs={{0,256},{256,0},{1,257},{257,1},{2,258},{258,2},{3,259},{259,3},{4... | collective-permute-start | bytes 1179656 | tf_op jit(solution)/shard_map/ppermute | solution.py:35
  86.9 22.9 %all-to-all-start.2 = ((bf16[16,32,768]{2,1,0:T(8,128)(2,1)}), bf16[16,32,768]{2,1,0:T(8,128)(2,1)S(1)}, u32[]{:S(2)}, u32[]{:S(2)}) async-start(bf16[16,32,768]{2,1,0:T(8,128)(2,1)} %broadcast_in_dim.10), calls=%async_computation.2 | async-start | bytes 1572864 | tf_op jit(solution)/shard_map/all_to_all | solution.py:22
  91.4 18.3 %copy-start.4 = (bf16[32,768]{1,0:T(8,128)(2,1)S(1)}, bf16[32,768]{1,0:T(8,128)(2,1)}, u32[]{:S(2)}) copy-start(bf16[32,768]{1,0:T(8,128)(2,1)} %get-tuple-element.17) | copy-start | bytes 147460
  110.6 16.7 %all-to-all-start.3 = ((bf16[8,32,768]{2,1,0:T(8,128)(2,1)}), bf16[8,32,768]{2,1,0:T(8,128)(2,1)}, u32[]{:S(2)}, u32[]{:S(2)}) async-start(bf16[8,32,768]{2,1,0:T(8,128)(2,1)} %broadcast_in_dim.11), calls=%async_computation.3 | async-start | bytes 786432 | tf_op jit(solution)/shard_map/all_to_all | solution.py:22
  117.9 19.8 %copy-start.3 = (bf16[16,2,16,768]{3,2,1,0:T(8,128)(2,1)S(1)}, bf16[16,2,16,768]{3,2,1,0:T(8,128)(2,1)}, u32[]{:S(2)}) copy-start(bf16[16,2,16,768]{3,2,1,0:T(8,128)(2,1)} %pad_maximum_fusion.1) | copy-start | bytes 2359300
  127.2 13.8 %collective-permute-start.3 = (bf16[256,768]{1,0:T(8,128)(2,1)}, bf16[256,768]{1,0:T(8,128)(2,1)S(1)}, u32[]{:S(2)}, u32[]{:S(2)}) collective-permute-start(bf16[256,768]{1,0:T(8,128)(2,1)} %bitcast.29), channel_id=1, source_target_pairs={{0,256},{256,0},{1,257},{257,1},{2,258},{258,2},{3,259},{259,3},{4... | collective-permute-start | bytes 1179656 | tf_op jit(solution)/shard_map/ppermute | solution.py:35
  130.3 18.9 %all-to-all-start.4 = ((bf16[16,16,768]{2,1,0:T(8,128)(2,1)}), bf16[16,16,768]{2,1,0:T(8,128)(2,1)S(1)}, u32[]{:S(2)}, u32[]{:S(2)}) async-start(bf16[16,16,768]{2,1,0:T(8,128)(2,1)} %bitcast.30), calls=%async_computation.4 | async-start | bytes 786432 | tf_op jit(solution)/shard_map/all_to_all | solution.py:22
  137.6 1.8 %copy-start.2 = (bf16[2,8,2,16,768]{4,3,2,1,0:T(8,128)(2,1)S(1)}, bf16[2,8,2,16,768]{4,3,2,1,0:T(8,128)(2,1)}, u32[]{:S(2)}) copy-start(bf16[2,8,2,16,768]{4,3,2,1,0:T(8,128)(2,1)} %pad_maximum_fusion.2) | copy-start | bytes 2359300
